TPU v7x, 32 devices: a whole 2x2x4 slice. The times are simulated.
32 devices in a mesh: ens: 2 (over x), space: 4 (over y, core), bin: 4 (over z).
Axes of the slice: x: 2, y: 2, z: 4, core: 2. Of those that a mesh axis runs over, the one named last changes fastest.
Arguments:
- spectrum: float32 [1296, 32768], P('bin', ('ens', 'space')), parts along dimension 1, may hold values from 0.05 to 1
- wind: float32 [2, 32768], P(None, ('ens', 'space')), parts along dimension 1, may hold values from -6 to 6
- sea_mask: int32 [16384], P('space'), may hold values 0 or 1
- neighbours: int32 [4, 16384], P(None, 'space'), may hold values from -4096 to 20479, as said below
- metric_x: float32 [16384], P('space'), may hold values from 0.05 to 0.3
- metric_y: float32 [16384], P('space'), may hold values from 0.05 to 0.3
- refraction: float32 [16384], P('space'), may hold values from -0.15 to 0.15
- freq_shift: float32 [16384], P('space'), may hold values from -0.15 to 0.15
- dia_bins: int32 [4, 1296], replicated, may hold values from 0 to 1295
- dia_wts: float32 [2, 1296], replicated, may hold values from 0 to 1
Outputs:
- spectrum_next: float32 [1296, 32768], P(None, ('ens', 'space', 'bin')), parts along dimension 1
There are 2 independent parts, one for each index of `ens`. A program takes and returns all parts, laid end to end along the dimension named above; an argument that names none is the same for every part. Nothing has to cross between parts.
Inputs may be any that keep to these rules, and one draw needn't show every extreme that they name: `neighbours`: row 0 is p + 1 to p + 3 and row 1 is p - 3 to p - 1 for point p; row 2 is p + k and row 3 is p - k with k from 2048 to 4096. Indices outside 0 to 16383 mean open boundary.
All inputs are finite; a program needn't handle non-finite values. No bound on the sum of `sea_mask` on one device may be relied on, other than what follows from the above.
Results may differ from a plain program's by a relative error of at most 0.0003.
Values sent between devices are 32-bit elements; how exact they have to be, the bound alone decides.
No kernel may reach another device: no remote copies, remote signals or barrier semaphores. Data moves between devices by JAX's collectives and lax.ppermute only.
A program may use at most 192 MiB of HBM per device.

v0:
```python
import functools
import itertools

import jax
import jax.numpy as jnp
import numpy as np
from jax import lax
from jax.experimental import pallas as pl
from jax.experimental.pallas import tpu as pltpu
from jax.sharding import PartitionSpec as P

ND = 36


def extended(array, sides, width):
    for axis, dim in sides:
        peers, length = (lax.axis_size(axis), array.shape[dim])
        up = [(i, (i + 1) % peers) for i in range(peers - 1)]
        down = [(j, i) for i, j in up]
        last = lax.slice_in_dim(array, length - width, length, axis=dim)
        initial = lax.slice_in_dim(array, 0, width, axis=dim)
        before = lax.ppermute(last, axis, up)
        after = lax.ppermute(initial, axis, down)
        array = jnp.concatenate([before, array, after], axis=dim)
    return array


def bin_tables(index, nfreq, ndir):
    freq = (index // ndir).astype(jnp.float32)
    direc = index % ndir
    fratio = jnp.exp(jnp.log(1.1) * (freq - (nfreq - 1)))
    speed = jnp.exp(-jnp.log(1.1) * freq)
    theta = 2.0 * jnp.pi * (direc.astype(jnp.float32) + 0.5) / ndir
    return (fratio, speed, jnp.cos(theta), jnp.sin(theta), direc == 0, direc == ndir - 1)


def spatial_term(wet, padded, local, metric_x, metric_y, speed, cosv, sinv):
    east = jnp.take(padded, local[0], axis=1)
    west = jnp.take(padded, local[1], axis=1)
    north = jnp.take(padded, local[2], axis=1)
    south = jnp.take(padded, local[3], axis=1)
    along_x = metric_x[None, :] * (speed * cosv)[:, None]
    along_y = metric_y[None, :] * (speed * sinv)[:, None]
    flux_x = jnp.abs(along_x) * (wet - jnp.where(along_x > 0, west, east))
    flux_y = jnp.abs(along_y) * (wet - jnp.where(along_y > 0, south, north))
    return flux_x + flux_y


def spectral_term(wet, padded, ndir, first, last, refraction, freq_shift, speed, cosv):
    rows = wet.shape[0]

    def moved_rows(offset):
        return lax.slice_in_dim(padded, ndir + offset, ndir + offset + rows, axis=0)

    prev_dir = jnp.where(first[:, None], moved_rows(ndir - 1), moved_rows(-1))
    next_dir = jnp.where(last[:, None], moved_rows(1 - ndir), moved_rows(1))
    lower = moved_rows(-ndir)
    upper = moved_rows(ndir)
    turning = refraction[None, :] * cosv[:, None]
    shifting = freq_shift[None, :] * speed[:, None]
    flux_t = jnp.abs(turning) * (wet - jnp.where(turning > 0, prev_dir, next_dir))
    flux_s = jnp.abs(shifting) * (wet - jnp.where(shifting > 0, lower, upper))
    return flux_t + flux_s


def source_step(
    moved, wind, maskf, fratio, speed, cosv, sinv, plus_fwd, minus_fwd, plus_back, minus_back
):
    steep = jnp.mean(moved * (fratio * fratio)[:, None], axis=0)
    drive = jnp.maximum(
        0.0,
        wind[0][None, :] * cosv[:, None] + wind[1][None, :] * sinv[:, None] - 0.5 * speed[:, None],
    )
    s_in = 0.3 * drive * drive * moved
    s_ds = -6.0 * fratio[:, None] * steep[None, :] * moved
    e_plus = plus_fwd(moved)
    e_minus = minus_fwd(moved)
    delta = (
        8.0
        * (fratio**4)[:, None]
        * (
            moved * moved * (e_plus / 1.25**4 + e_minus / 0.75**4)
            - 2.0 * moved * e_plus * e_minus / 0.9375**4
        )
    )
    s_nl = -2.0 * delta + plus_back(delta) + minus_back(delta)
    return (moved + 0.5 * (s_in + s_ds + s_nl)) * maskf[None, :]


def pair_matrix(first_bins, second_bins, weight, count):
    columns = jnp.arange(count, dtype=jnp.int32)[None, :]
    return weight[:, None] * (first_bins[:, None] == columns).astype(jnp.float32) + (1.0 - weight)[
        :, None
    ] * (second_bins[:, None] == columns).astype(jnp.float32)


def forward_product(matrix, values):
    return jnp.dot(
        matrix, values, precision=lax.Precision.HIGHEST, preferred_element_type=jnp.float32
    )


def backward_product(matrix, values):
    return lax.dot_general(
        matrix,
        values,
        (((0,), (0,)), ((), ())),
        precision=lax.Precision.HIGHEST,
        preferred_element_type=jnp.float32,
    )


def on_device(
    spectrum,
    wind,
    sea_mask,
    neighbours,
    metric_x,
    metric_y,
    refraction,
    freq_shift,
    dia_bins,
    dia_wts,
):
    bins_dev, points_dev = spectrum.shape
    nbins = dia_bins.shape[1]
    ndir = ND
    nfreq = nbins // ndir
    space_pos = lax.axis_index("space")
    bin_pos = lax.axis_index("bin")
    maskf = sea_mask.astype(jnp.float32)
    wet = spectrum * maskf[None, :]
    padded = extended(wet, (("space", 1),), points_dev)
    base = space_pos * points_dev - points_dev
    local = neighbours - base
    own_bins = bin_pos * bins_dev + jnp.arange(bins_dev, dtype=jnp.int32)
    fratio, speed, cosv, sinv, first, last = bin_tables(own_bins, nfreq, ndir)
    spatial = spatial_term(wet, padded, local, metric_x, metric_y, speed, cosv, sinv)
    share = points_dev // lax.axis_size("bin")
    start = bin_pos * share
    all_bins = jnp.arange(nbins, dtype=jnp.int32)
    fratio_all, speed_all, cos_all, sin_all, first_all, last_all = bin_tables(all_bins, nfreq, ndir)
    bin_pad = extended(wet, (("bin", 0),), ndir)
    spectral = spectral_term(wet, bin_pad, ndir, first, last, refraction, freq_shift, speed, cosv)
    moved_own = wet - spatial - spectral
    moved = lax.all_to_all(moved_own, "bin", split_axis=1, concat_axis=0, tiled=True)
    wind_part = lax.dynamic_slice_in_dim(wind, start, share, 1)
    mask_part = lax.dynamic_slice_in_dim(maskf, start, share, 0)
    plus_matrix = pair_matrix(dia_bins[0], dia_bins[1], dia_wts[0], nbins)
    minus_matrix = pair_matrix(dia_bins[2], dia_bins[3], dia_wts[1], nbins)
    result = source_step(
        moved,
        wind_part,
        mask_part,
        fratio_all,
        speed_all,
        cos_all,
        sin_all,
        lambda v: forward_product(plus_matrix, v),
        lambda v: forward_product(minus_matrix, v),
        lambda v: backward_product(plus_matrix, v),
        lambda v: backward_product(minus_matrix, v),
    )
    return result


LANES = 128
ROWS = 8
EDGE = 16
QUART = ND // 4
APART = 3
PIECES = 6
VMEM_ASK = 60 << 20
GROUP = 4


def chunk_plan(nloc):
    mid = nloc // 2
    plan = [(mid - d, 2 * d, 2) for d in range(1, mid + 1)]
    if mid > 3:
        plan[2] = (mid - 3, 3, 3)
    else:
        plan.insert(0, (mid, 1, 1))
    return plan


def freqs_of(chunk):
    first, step, count = chunk
    return [first + i * step for i in range(count)]


def halo_groups(plan):
    return [g for g in (plan[:1], plan[1:]) if g]


def slots_of(group):
    return {f: i for i, f in enumerate(f for chunk in group for f in freqs_of(chunk))}


def runs_of(freqs):
    runs = []
    for f in sorted(freqs):
        if runs and runs[-1][1] == f:
            runs[-1] = (runs[-1][0], f + 1)
        else:
            runs.append((f, f + 1))
    return runs


def prep_kernel(points, bins, blocks, groups, full, spec_hbm, mask_ref, *refs):
    ngr = len(groups)
    nloc = bins // ND
    hs_hbm, hn_hbm = refs[:ngr], refs[ngr : 2 * ngr]
    if full:
        wet_hbm, low_hbm, high_hbm = refs[2 * ngr : 2 * ngr + 3]
    spec_v, wet_v, edge_v, in_sem, out_sem = refs[-5:]
    tiles = points // LANES
    half = ND // 2
    where = {f: (i, k) for i, group in enumerate(groups) for f, k in slots_of(group).items()}
    loads = []
    spans = []
    for lo, hi in blocks:
        start = lo * ND // ROWS * ROWS
        stop = min(-(-hi * ND // ROWS) * ROWS, bins)
        spans.append((start, stop))
        rows = pl.ds(start, stop - start)
        copy = pltpu.make_async_copy(spec_hbm.at[rows], spec_v.at[rows], in_sem.at[len(loads)])
        copy.start()
        loads.append(copy)
    masks = [mask_ref[:, c * LANES : (c + 1) * LANES].astype(jnp.float32) for c in range(tiles)]
    copies = []

    def send(src, dst):
        copy = pltpu.make_async_copy(src, dst, out_sem.at[len(copies)])
        copy.start()
        copies.append(copy)

    for (lo, hi), (start, stop), load in zip(blocks, spans, loads):
        load.wait()

        def turn(g0, count):
            for c0 in range(0, tiles, ROWS):
                cols = range(c0, c0 + ROWS)
                block = jnp.stack(
                    [spec_v[pl.ds(g0, count), c * LANES : (c + 1) * LANES] * masks[c] for c in cols], axis=0
                )
                block = jnp.swapaxes(block, 0, 1)
                for i in range(count):
                    wet_v[pl.ds(pl.multiple_of((g0 + i) * tiles + c0, ROWS), ROWS), :] = block[i]

        def relayout(t, _):
            turn(pl.multiple_of(start + t * ROWS, ROWS), ROWS)
            return 0

        lax.fori_loop(0, (stop - start) // ROWS, relayout, 0)
        rest = (stop - start) % ROWS
        if rest:
            g0 = stop - rest
            for c in range(tiles):
                tile = spec_v[pl.ds(g0, rest), c * LANES : (c + 1) * LANES]
                wet_v[pl.ds(g0 * tiles + c, rest, stride=tiles), :] = tile * masks[c]
        for f in range(lo, hi):
            base = f * ND * tiles
            if f in where:
                i, k = where[f]
                for side, (j0, row) in enumerate(((3 * QUART, tiles - 1), (QUART, 0))):
                    at = base + j0 * tiles + row
                    edge_v[f, side, ROWS:EDGE, :] = jnp.zeros((EDGE - ROWS, LANES), jnp.float32)
                    edge_v[f, side, 0:ROWS, :] = wet_v[pl.ds(at, ROWS, stride=tiles), :]
                    edge_v[f, side, ROWS : ROWS + 1, :] = wet_v[pl.ds(at + ROWS * tiles, 1), :]
                span = half * tiles
                send(wet_v.at[pl.ds(base, span)], hs_hbm[i].at[k, pl.ds(0, span)])
                send(wet_v.at[pl.ds(base + span, span)], hn_hbm[i].at[k, pl.ds(0, span)])
                send(edge_v.at[f, 0], hs_hbm[i].at[k, pl.ds(span, EDGE)])
                send(edge_v.at[f, 1], hn_hbm[i].at[k, pl.ds(span, EDGE)])
            if full:
                own = pl.ds(base, ND * tiles)
                if f == nloc - 1:
                    send(wet_v.at[own], low_hbm)
                if f == 0:
                    send(wet_v.at[own], high_hbm)
                send(wet_v.at[own], wet_hbm.at[own])
    for copy in copies:
        copy.wait()


def prep(spectrum, mask, blocks, groups, full):
    bins, points = spectrum.shape
    nloc = bins // ND
    tiles = points // LANES
    halo_rows = ND // 2 * tiles + EDGE
    halos = [jax.ShapeDtypeStruct((len(slots_of(g)), halo_rows, LANES), jnp.float32) for g in groups]
    one = jax.ShapeDtypeStruct((ND * tiles, LANES), jnp.float32)
    outs = halos + halos
    if full:
        outs += [jax.ShapeDtypeStruct((bins * tiles, LANES), jnp.float32), one, one]
    anywhere = pl.BlockSpec(memory_space=pl.ANY)
    count = sum(hi - lo for lo, hi in blocks)
    sends = 4 * sum(len(slots_of(g)) for g in groups) + (nloc + 2 if full else 0)
    res = pl.pallas_call(
        functools.partial(prep_kernel, points, bins, blocks, groups, full),
        out_shape=outs,
        in_specs=[anywhere, pl.BlockSpec(memory_space=pltpu.VMEM)],
        out_specs=[anywhere] * len(outs),
        scratch_shapes=[
            pltpu.VMEM((bins, points), jnp.float32),
            pltpu.VMEM((bins * tiles, LANES), jnp.float32),
            pltpu.VMEM((nloc, 2, EDGE, LANES), jnp.float32),
            pltpu.SemaphoreType.DMA((len(blocks),)),
            pltpu.SemaphoreType.DMA((sends,)),
        ],
        compiler_params=pltpu.CompilerParams(vmem_limit_bytes=VMEM_ASK),
        cost_estimate=pl.CostEstimate(flops=0, bytes_accessed=count * 3_000_000, transcendentals=0),
        name="prep",
    )(spectrum, mask)
    ngr = len(groups)
    return res[:ngr], res[ngr : 2 * ngr], res[2 * ngr :]


def front_kernel(
    tiles, shares, nloc, kmin, kmax, chunk, edge, joined, tab_ref, dir_ref, pos_ref, nbr_ref, mx_ref, my_ref, rf_ref, fs_ref, hs_ref, hn_ref, wet_ref, *refs
):
    nout = 1 if joined else shares
    near, outs, ext_ref = refs[: -nout - 1], refs[-nout - 1 : -1], refs[-1]
    if joined:
        outs = [outs[0].at[d] for d in range(shares)]
    place = pl.program_id(0)
    speed = tab_ref[pos_ref[0] * nloc + chunk[0] + chunk[1] * place]
    first = place == 0
    half = ND // 2
    span = half * tiles
    south, north = tiles, ROWS
    pitch = APART * (2 * tiles + ROWS)

    def rows_at(j, row, count=ROWS):
        return pl.ds(j * pitch + APART * row, count, stride=APART)

    def extend(q, _):
        for t in range(0, tiles, ROWS):
            ext_ref[rows_at(q, t), :] = hs_ref[0, pl.ds(pl.multiple_of(q * tiles + t, ROWS), ROWS), :]
            ext_ref[rows_at(q, south + t), :] = wet_ref[0, q, t : t + ROWS, :]
            ext_ref[rows_at(half + q, north + t), :] = wet_ref[0, half + q, t : t + ROWS, :]
            ext_ref[rows_at(half + q, north + tiles + t), :] = hn_ref[
                0, pl.ds(pl.multiple_of(q * tiles + t, ROWS), ROWS), :
            ]
        return 0

    lax.fori_loop(0, half, extend, 0, unroll=2)
    for q in range(QUART):
        ext_ref[pl.ds((QUART + q) * pitch + APART * (south + tiles), 1), :] = hn_ref[0, span + q : span + q + 1, :]
        ext_ref[pl.ds((3 * QUART + q) * pitch + APART * (north - 1), 1), :] = hs_ref[0, span + q : span + q + 1, :]

    side = jnp.where(first, 1.0, -1.0)
    per_share = tiles // shares
    steps = [(d, k) for d in range(shares) for k in range(per_share // ROWS)]
    firsts = {}
    for d, k in steps:
        row = (d if joined else lax.rem(pos_ref[0] + d, shares)) * per_share + k * ROWS
        firsts[d, k] = row if joined else pl.multiple_of(row, ROWS)
    sub = lax.broadcasted_iota(jnp.int32, (ROWS, LANES), 0)
    lanes, rels = {}, {}
    for way in range(4):
        for step in steps:
            src = nbr_ref[way, pl.ds(firsts[step], ROWS), :]
            lanes[way, step] = src & (LANES - 1)
            rels[way, step] = (src >> 7) - (sub + firsts[step])

    def picked(j, own, step, way, offsets):
        out = None
        for r in offsets:
            window = ext_ref[rows_at(j, own + firsts[step] + r), :]
            got = jnp.take_along_axis(window, lanes[way, step], axis=1, mode="promise_in_bounds")
            out = got if out is None else jnp.where(rels[way, step] == r, got, out)
        return out

    for quad in range(4):
        cos_up = quad in (0, 3)
        own, way_y, off_y = (
            (south, 3, range(-(kmax // LANES), -(kmin // LANES) + 1))
            if quad < 2
            else (north, 2, range(kmin // LANES, kmax // LANES + 1))
        )
        way_x, off_x = (1, (-1, 0)) if cos_up else (0, (0, 1))

        def body(q, _):
            j = quad * QUART + q
            jprev = jnp.where(j == 0, ND - 1, j - 1)
            jnext = jnp.where(j == ND - 1, 0, j + 1)
            acos = jnp.abs(dir_ref[0, j])
            asin = jnp.abs(dir_ref[1, j])
            ax, ay = speed * acos, speed * asin
            for step in steps:
                at = pl.ds(firsts[step], ROWS)
                wet = wet_ref[0, j, at, :]
                e_y = picked(j, own, step, way_y, off_y)
                e_x = picked(j, own, step, way_x, off_x)
                rf, fs = rf_ref[at, :], fs_ref[at, :]
                e_prev, e_next = wet_ref[0, jprev, at, :], wet_ref[0, jnext, at, :]
                e_t = jnp.where(rf > 0, e_prev, e_next) if cos_up else jnp.where(rf < 0, e_prev, e_next)
                if edge:
                    inner, low, high = (ref[0, j, at, :] for ref in near)
                    outer = jnp.where(first, low, high)
                    e_s = jnp.where(fs * side > 0, outer, inner)
                else:
                    e_s = jnp.where(fs > 0, near[0][0, j, at, :], near[1][0, j, at, :])
                spatial = (mx_ref[at, :] * ax) * (wet - e_x) + (my_ref[at, :] * ay) * (wet - e_y)
                spectral = (jnp.abs(rf) * acos) * (wet - e_t) + (jnp.abs(fs) * speed) * (wet - e_s)
                d, k = step
                outs[d][j, k * ROWS : (k + 1) * ROWS, :] = wet - spatial - spectral
            return 0

        lax.fori_loop(0, QUART, body, 0, unroll=3)


def front(speed, dirs, pos, nbr, par, hs, hn, slot, wet, ends, chunk, joined, shares, kmin, kmax):
    first, step, count = chunk
    tiles = nbr.shape[1]
    nloc = wet.shape[0]
    smem = pl.BlockSpec(memory_space=pltpu.SMEM)

    def freq_spec(start, step):
        return pl.BlockSpec((1, ND, tiles, LANES), lambda i: (start + i * step, 0, 0, 0))

    halo_spec = pl.BlockSpec((1,) + hs.shape[1:], lambda i: (slot + i, 0, 0))

    def whole(shape):
        return pl.BlockSpec(shape, lambda i: (0,) * len(shape))

    if ends:
        near, near_specs = (wet,) + ends, [freq_spec(1, nloc - 3), freq_spec(0, 0), freq_spec(0, 0)]
    else:
        near, near_specs = (wet, wet), [freq_spec(first - 1, step), freq_spec(first + 1, step)]
    rows = tiles // shares
    if joined:
        outs = [jax.ShapeDtypeStruct((shares, count * ND, rows, LANES), jnp.float32)]
        out_specs = [pl.BlockSpec((shares, ND, rows, LANES), lambda i: (0, i, 0, 0))]
    else:
        outs = [jax.ShapeDtypeStruct((count * ND, rows, LANES), jnp.float32)] * shares
        out_specs = [pl.BlockSpec((ND, rows, LANES), lambda i: (i, 0, 0))] * shares
    return pl.pallas_call(
        functools.partial(front_kernel, tiles, shares, nloc, kmin, kmax, chunk, bool(ends), joined),
        grid=(count,),
        out_shape=outs,
        in_specs=[smem] * 3
        + [whole(nbr.shape)] + [whole(p.shape) for p in par] + [halo_spec, halo_spec, freq_spec(first, step)]
        + near_specs,
        out_specs=out_specs,
        scratch_shapes=[pltpu.VMEM((ND * APART * (2 * tiles + ROWS), LANES), jnp.float32)],
        compiler_params=pltpu.CompilerParams(vmem_limit_bytes=VMEM_ASK),
        cost_estimate=pl.CostEstimate(flops=0, bytes_accessed=count * 22_000_000, transcendentals=0),
        name="front",
    )(speed, dirs, pos, nbr, *par, hs, hn, wet, *near)


def tail_kernel(nfreq, bins_dev, plan, spot_ref, wts_ref, ftab_ref, frs_ref, dir_ref, pos_ref, wind_ref, mask_ref, *refs):
    out_hbm, mv, base, a0, a1, a2, a3, dw, out_v, in_sem, out_sem = refs[-11:]
    parts = iter(refs[:-11])
    shares = nfreq * ND // bins_dev
    nbins = nfreq * ND
    loads = []
    for c, chunk in enumerate(plan):
        joined = c == 0
        whole = next(parts) if joined else None
        for d in range(shares):
            part = whole.at[d] if joined else next(parts)
            source = d if joined else lax.rem(pos_ref[0] + (shares - d), shares)
            for i, f in enumerate(freqs_of(chunk)):
                rows = pl.ds(source * bins_dev + f * ND, ND)
                copy = pltpu.make_async_copy(part.at[pl.ds(i * ND, ND)], mv.at[rows], in_sem.at[len(loads)])
                copy.start()
                loads.append(copy)
    zero = jnp.zeros((ROWS, LANES), jnp.float32)
    accs = (a0, a1, a2, a3)

    def clear(g, _):
        for acc in accs:
            acc[g] = zero
        return 0

    lax.fori_loop(0, nbins, clear, 0, unroll=8)
    for j in range(ND):
        dw[j] = wind_ref[0] * dir_ref[0, j] + wind_ref[1] * dir_ref[1, j]
    for copy in loads:
        copy.wait()

    def per_freq(f, steep):
        fr2, fr4, hspeed = ftab_ref[0, f], ftab_ref[1, f], ftab_ref[2, f]

        def per_group(t, total):
            j0 = t * GROUP
            g0 = f * ND + j0
            spots = [[spot_ref[4 * g0 + 4 * i + k] for k in range(4)] for i in range(GROUP)]
            own = [mv[g0 + i] for i in range(GROUP)]
            found = [[mv[b] for b in spots[i]] for i in range(GROUP)]
            adds = []
            for i in range(GROUP):
                m, (p0, p1, m0, m1) = own[i], found[i]
                wp, wm = wts_ref[2 * g0 + 2 * i], wts_ref[2 * g0 + 2 * i + 1]
                ep = p1 + wp * (p0 - p1)
                em = m1 + wm * (m0 - m1)
                mf = fr4 * m
                half = mf * (m * (ep * (1 / 1.25**4) + em * (1 / 0.75**4)) - ep * em * (2.0 / 0.9375**4))
                drive = jnp.maximum(0.0, dw[j0 + i] - hspeed)
                base[g0 + i] = m + 0.15 * (drive * drive) * m - 2.0 * half
                sp, sm = wp * half, wm * half
                adds.append((sp, half - sp, sm, half - sm))
                total = total + m
            for i in range(0, GROUP, 2):
                for acc, b0, b1, x0, x1 in zip(accs, spots[i], spots[i + 1], adds[i], adds[i + 1]):
                    old0, old1 = acc[b0], acc[b1]
                    acc[b0] = old0 + x0
                    acc[b1] = old1 + (x1 + jnp.where(b0 == b1, x0, zero))
            return total

        return steep + lax.fori_loop(0, ND // GROUP, per_group, zero, unroll=3) * fr2

    steep = lax.fori_loop(0, nfreq, per_freq, zero)
    steep = steep * (1.0 / nbins)
    mask = mask_ref[...].astype(jnp.float32)
    per = nbins // PIECES
    copies = []
    for p in range(PIECES):

        def finish(t, _):
            g0 = t * ROWS
            done = []
            for i in range(ROWS):
                g = g0 + i
                mine = base[g] - (frs_ref[g] * steep) * mv[g]
                done.append((mine + ((a0[g] + a1[g]) + (a2[g] + a3[g]))) * mask)
            turned = jnp.swapaxes(jnp.stack(done, axis=0), 0, 1)
            for c in range(ROWS):
                out_v[pl.ds(pl.multiple_of(g0, ROWS), ROWS), c * LANES : (c + 1) * LANES] = turned[c]
            return 0

        lax.fori_loop(p * per // ROWS, (p + 1) * per // ROWS, finish, 0, unroll=3)
        rows = pl.ds(p * per, per)
        copy = pltpu.make_async_copy(out_v.at[rows], out_hbm.at[rows], out_sem.at[p])
        copy.start()
        copies.append(copy)
    for copy in copies:
        copy.wait()


def tail(parts, plan, bins_dev, dia_bins, dia_wts, ftab, frs, dirs, pos, wind, mask):
    nbins = dia_bins.shape[1]
    nfreq = nbins // ND
    anywhere = pl.BlockSpec(memory_space=pl.ANY)
    smem = pl.BlockSpec(memory_space=pltpu.SMEM)
    vmem = pl.BlockSpec(memory_space=pltpu.VMEM)
    points = ROWS * LANES
    spots = dia_bins.T.reshape(-1)
    wts = dia_wts.T.reshape(-1)
    field = pltpu.VMEM((nbins, ROWS, LANES), jnp.float32)
    return pl.pallas_call(
        functools.partial(tail_kernel, nfreq, bins_dev, plan),
        out_shape=jax.ShapeDtypeStruct((nbins, points), jnp.float32),
        in_specs=[smem] * 6 + [vmem] * 2 + [anywhere] * len(parts),
        out_specs=anywhere,
        scratch_shapes=[field] * 6
        + [
            pltpu.VMEM((ND, ROWS, LANES), jnp.float32),
            pltpu.VMEM((nbins, points), jnp.float32),
            pltpu.SemaphoreType.DMA((nbins // ND,)),
            pltpu.SemaphoreType.DMA((PIECES,)),
        ],
        compiler_params=pltpu.CompilerParams(vmem_limit_bytes=VMEM_ASK),
        cost_estimate=pl.CostEstimate(flops=0, bytes_accessed=70_000_000, transcendentals=0),
        name="tail",
    )(spots, wts, ftab, frs, dirs, pos, wind, mask, *parts)


def fast_on_device(
    spectrum, wind, sea_mask, neighbours, metric_x, metric_y, refraction, freq_shift, dia_bins, dia_wts
):
    bins_dev, points = spectrum.shape
    nbins = dia_bins.shape[1]
    nfreq = nbins // ND
    nloc = bins_dev // ND
    tiles = points // LANES
    shares = lax.axis_size("bin")
    share = points // shares
    bin_pos = lax.axis_index("bin")
    space_pos = lax.axis_index("space")
    plan = chunk_plan(nloc)

    freqs = np.arange(nfreq, dtype=np.float32)
    speed = jnp.asarray(np.exp(-np.log(1.1) * freqs.astype(np.float64)).astype(np.float32))
    ratio = np.exp(np.log(1.1) * (freqs.astype(np.float64) - (nfreq - 1)))
    ftab = jnp.asarray(
        np.stack([ratio**2, 4.0 * ratio**4, 0.5 * np.exp(-np.log(1.1) * freqs)]).astype(np.float32)
    )
    frs = jnp.asarray(np.repeat(3.0 * ratio, ND).astype(np.float32))
    theta = 2.0 * np.pi * (np.arange(ND) + 0.5) / ND
    dirs = jnp.asarray(np.stack([np.cos(theta), np.sin(theta)]).astype(np.float32))

    groups = halo_groups(plan)
    early = runs_of(slots_of(groups[0]))
    mask_row = sea_mask.reshape(1, points)
    hs, hn, _ = prep(spectrum, mask_row, early, groups[:1], False)
    after, *_ = lax.optimization_barrier((spectrum, hs[0], hn[0]))
    whole_blocks = [(f, min(f + 2, nloc)) for f in range(0, nloc, 2)]
    hs_rest, hn_rest, (wet, low_out, high_out) = prep(after, mask_row, whole_blocks, groups[1:], True)
    wet = wet.reshape(nloc, ND, tiles, LANES)

    def line(array, axis, step):
        peers = lax.axis_size(axis)
        pairs = [(i, i + 1) for i in range(peers - 1)]
        if step < 0:
            pairs = [(b, a) for a, b in pairs]
        return lax.ppermute(array, axis, pairs)

    sends = list(zip(list(hs) + list(hs_rest), list(hn) + list(hn_rest)))
    halos = []

    def send_halos(*after):
        if len(halos) < len(sends):
            south, north = sends[len(halos)]
            if after:
                south, north, *_ = lax.optimization_barrier((south, north) + after)
            halos.append((line(south, "space", 1), line(north, "space", -1)))

    send_halos()
    send_halos(*halos[0])
    low_in = line(low_out, "bin", 1).reshape(1, ND, tiles, LANES)
    high_in = line(high_out, "bin", -1).reshape(1, ND, tiles, LANES)

    nbr = (neighbours - space_pos * points).reshape(4, tiles, LANES)
    par = [p.reshape(tiles, LANES) for p in (metric_x, metric_y, refraction, freq_shift)]
    pos = bin_pos.reshape(1)
    kmin, kmax = points // 2, points
    arrived = []
    order = pos
    for c, chunk in enumerate(plan):
        first, step, count = chunk
        joined = c == 0
        gi, slot = [(i, slots_of(g)[first]) for i, g in enumerate(groups) if chunk in g][0]
        ends = (low_in, high_in) if first == 0 else None
        blocks = front(speed, dirs, order, nbr, par, *halos[gi], slot, wet, ends, chunk, joined, shares, kmin, kmax)
        earlier = sum(halos, ()) if c == 0 else arrived[0] if c == 1 else []
        order, *_ = lax.optimization_barrier((pos, blocks[0], *earlier))
        if joined:
            arrived.append([lax.all_to_all(blocks[0], "bin", split_axis=0, concat_axis=0, tiled=True)])
            continue
        here = [blocks[0]]
        for d in range(1, shares):
            rows = blocks[d]
            if c > 1:
                rows, _ = lax.optimization_barrier((rows, arrived[-1][d]))
            here.append(lax.ppermute(rows, "bin", [(i, (i + d) % shares) for i in range(shares)]))
        arrived.append(here)
    parts = sum(arrived, [])
    wind_part = lax.dynamic_slice_in_dim(wind, bin_pos * share, share, 1).reshape(2, ROWS, LANES)
    mask_part = lax.dynamic_slice_in_dim(sea_mask, bin_pos * share, share, 0).reshape(ROWS, LANES)
    return tail(parts, plan, bins_dev, dia_bins, dia_wts, ftab, frs, dirs, pos, wind_part, mask_part)


def pick_path(spectrum, *others):
    bins_dev, points = spectrum.shape
    fits = bins_dev % (2 * ND) == ND and bins_dev > ND and points // lax.axis_size("bin") == ROWS * LANES
    return (fast_on_device if fits else on_device)(spectrum, *others)


def solution(mesh):
    return jax.shard_map(
        pick_path,
        mesh=mesh,
        in_specs=(
            P("bin", ("ens", "space")),
            P(None, ("ens", "space")),
            P("space"),
            P(None, "space"),
            P("space"),
            P("space"),
            P("space"),
            P("space"),
            P(),
            P(),
        ),
        out_specs=P(None, ("ens", "space", "bin")),
        check_vma=False,
    )
```

profile of v0, /device:TPU:1, one launch (start us, length us, event | category | flops | bytes accessed | tf_op | source)
XLA Modules:
  0.0 195.9 jit_solution(15033703116475958287)
XLA Ops:
  0.0 0.0 copy-start
  0.0 3.2 %prep.2 = (f32[2,592,128]{2,1,0:T(8,128)}, f32[2,592,128]{2,1,0:T(8,128)}) custom-call(f32[324,4096]{1,0:T(8,128)} %spec_hbm.2, s32[1,4096]{1,0:T(1,128)} %bitcast.56), custom_call_target="tpu_custom_call" | custom-call | bytes 6000000 | tf_op jit(solution)/shard_map/prep/pallas_call | solution.py:300
  3.2 4.5 %collective-permute-start = (f32[2,592,128]{2,1,0:T(8,128)}, f32[2,592,128]{2,1,0:T(8,128)S(1)}, u32[]{:S(2)}, u32[]{:S(2)}) collective-permute-start(f32[2,592,128]{2,1,0:T(8,128)} %get-tuple-element.36), channel_id=1, source_target_pairs={{0,4},{4,8},{8,12},{1,5},{5,9},{9,13},{2,6},{6,10},{10,14},{3,7},{... | collective-permute-start | bytes 1818632 | tf_op jit(solution)/shard_map/ppermute | solution.py:611
  7.7 0.0 copy-start.15
  7.7 2.1 %collective-permute-start.1 = (f32[2,592,128]{2,1,0:T(8,128)}, f32[2,592,128]{2,1,0:T(8,128)S(1)}, u32[]{:S(2)}, u32[]{:S(2)}) collective-permute-start(f32[2,592,128]{2,1,0:T(8,128)} %get-tuple-element.37), channel_id=1, source_target_pairs={{4,0},{8,4},{12,8},{5,1},{9,5},{13,9},{6,2},{10,6},{14,10},{7,3},{... | collective-permute-start | bytes 1818632 | tf_op jit(solution)/shard_map/ppermute | solution.py:611
  9.8 6.8 %prep.3 = (f32[7,592,128]{2,1,0:T(8,128)}, f32[7,592,128]{2,1,0:T(8,128)}, f32[10368,128]{1,0:T(8,128)}, f32[1152,128]{1,0:T(8,128)}, f32[1152,128]{1,0:T(8,128)}) custom-call(f32[324,4096]{1,0:T(8,128)} %spec_hbm.2, s32[1,4096]{1,0:T(1,128)} %bitcast.57), custom_call_target="tpu_custom_call" | custom-call | bytes 27000000 | tf_op jit(solution)/shard_map/prep/pallas_call | solution.py:300
  16.5 0.0 collective-permute-done.hs_ref
  16.6 0.0 copy-start.3
  16.6 2.9 %collective-permute-done.1.hn_ref = f32[2,592,128]{2,1,0:T(8,128)S(1)} collective-permute-done((f32[2,592,128]{2,1,0:T(8,128)}, f32[2,592,128]{2,1,0:T(8,128)S(1)}, u32[]{:S(2)}, u32[]{:S(2)}) %collective-permute-start.1) | collective-permute-done | bytes 606240 | tf_op jit(solution)/shard_map/ppermute | solution.py:611
  19.4 1.9 collective-permute-start.2
  21.4 2.5 %collective-permute-start.3 = (f32[7,592,128]{2,1,0:T(8,128)}, f32[7,592,128]{2,1,0:T(8,128)}, u32[]{:S(2)}, u32[]{:S(2)}) collective-permute-start(f32[7,592,128]{2,1,0:T(8,128)} %get-tuple-element.43), channel_id=1, source_target_pairs={{4,0},{8,4},{12,8},{5,1},{9,5},{13,9},{6,2},{10,6},{14,10},{7,3},{... | collective-permute-start | bytes 6365192 | tf_op jit(solution)/shard_map/ppermute | solution.py:611
  23.9 0.0 copy-done.15
  23.9 0.6 copy.21
  24.6 0.0 copy-done.3
  24.6 0.0 copy-done.4
  24.6 12.6 %front.4 = f32[4,72,8,128]{3,2,1,0:T(8,128)} custom-call(f32[36]{0:T(128)} %constant.21.clone.tab_ref, f32[2,36]{1,0:T(2,128)} %constant.24.clone.dir_ref, s32[1]{0:T(128)} %bitcast.2.pos_ref, s32[4,32,128]{2,1,0:T(8,128)} %bitcast.34, f32[32,128]{1,0:T(8,128)} %bitcast.40, f32[32,128]{1,0:T(8,128)} %bitcast.44, f32[32,128]{1,0:T(8,128)} %bitcast.48, ...), custom_call_target="tpu_custom_call" | custom-call | bytes 44000000 | tf_op jit(solution)/shard_map/front/pallas_call | solution.py:440
  37.1 4.6 %all-to-all-start = ((f32[4,72,8,128]{3,2,1,0:T(8,128)}), f32[4,72,8,128]{3,2,1,0:T(8,128)S(1)}, u32[]{:S(2)}, u32[]{:S(2)}) async-start(f32[4,72,8,128]{3,2,1,0:T(8,128)} %front.4), calls=%async_computation | async-start | bytes 2359296 | tf_op jit(solution)/shard_map/all_to_all | solution.py:643
  41.7 3.2 %collective-permute-done.2.hs_ref = f32[7,592,128]{2,1,0:T(8,128)S(1)} collective-permute-done((f32[7,592,128]{2,1,0:T(8,128)}, f32[7,592,128]{2,1,0:T(8,128)S(1)}, u32[]{:S(2)}, u32[]{:S(2)}) %collective-permute-start.2) | collective-permute-done | bytes 2121760 | tf_op jit(solution)/shard_map/ppermute | solution.py:611
  44.9 4.6 %collective-permute-done.3.hn_ref = f32[7,592,128]{2,1,0:T(8,128)} collective-permute-done((f32[7,592,128]{2,1,0:T(8,128)}, f32[7,592,128]{2,1,0:T(8,128)}, u32[]{:S(2)}, u32[]{:S(2)}) %collective-permute-start.3) | collective-permute-done | bytes 2121760 | tf_op jit(solution)/shard_map/ppermute | solution.py:611
  49.5 0.0 copy-done.1
  49.5 12.8 %front.5 = (f32[72,8,128]{2,1,0:T(8,128)}, f32[72,8,128]{2,1,0:T(8,128)}, f32[72,8,128]{2,1,0:T(8,128)}, f32[72,8,128]{2,1,0:T(8,128)}) custom-call(f32[36]{0:T(128)} %constant.21.clone.tab_ref, f32[2,36]{1,0:T(2,128)} %constant.24.clone.dir_ref, s32[1]{0:T(128)} %bitcast.2.pos_ref, s32[4,32,128]{2,1,0:T(8,128)} %bitcast.35, f32[32,128]{1,0:T(8,128)} %bitcast.41, ...), custom_call_target="tpu_custom_call" | custom-call | bytes 44000000 | tf_op jit(solution)/shard_map/front/pallas_call | solution.py:440
  62.2 3.4 %collective-permute-start.6 = (f32[72,8,128]{2,1,0:T(8,128)}, f32[72,8,128]{2,1,0:T(8,128)S(1)}, u32[]{:S(2)}, u32[]{:S(2)}) collective-permute-start(f32[72,8,128]{2,1,0:T(8,128)} %get-tuple-element.48), channel_id=1, source_target_pairs={{0,3},{1,0},{2,1},{3,2},{4,7},{5,4},{6,5},{7,6},{8,11},{9,8},{10,9... | collective-permute-start | bytes 884744 | tf_op jit(solution)/shard_map/ppermute | solution.py:650
  65.6 0.0 collective-permute-start.5
  65.6 0.5 collective-permute-start.4
  66.1 4.1 %collective-permute-start.10 = (f32[1152,128]{1,0:T(8,128)}, f32[1152,128]{1,0:T(8,128)S(1)}, u32[]{:S(2)}, u32[]{:S(2)}) collective-permute-start(f32[1152,128]{1,0:T(8,128)} %get-tuple-element.58), channel_id=1, source_target_pairs={{0,1},{1,2},{2,3},{4,5},{5,6},{6,7},{8,9},{9,10},{10,11},{12,13},{... | collective-permute-start | bytes 1769480 | tf_op jit(solution)/shard_map/ppermute | solution.py:611
  70.2 1.3 collective-permute-start.11
  71.5 0.0 all-to-all-done.refs_0_
  71.5 0.0 copy-start.2
  71.5 18.2 %front.6 = (f32[108,8,128]{2,1,0:T(8,128)}, f32[108,8,128]{2,1,0:T(8,128)}, f32[108,8,128]{2,1,0:T(8,128)}, f32[108,8,128]{2,1,0:T(8,128)}) custom-call(f32[36]{0:T(128)} %constant.21.clone.tab_ref, f32[2,36]{1,0:T(2,128)} %constant.24.clone.dir_ref, s32[1]{0:T(128)} %bitcast.2.pos_ref, s32[4,32,128]{2,1,0:T(8,128)} %bitcast.36, f32[32,128]{1,0:T(8,128)} %bitcast.42, ...), custom_call_target="tpu_custom_call" | custom-call | bytes 66000000 | tf_op jit(solution)/shard_map/front/pallas_call | solution.py:440
  89.7 0.0 copy-done.2
  89.7 0.0 collective-permute-done.6.refs_4_
  89.7 0.0 copy-start.10
  89.8 0.7 copy-done.10
  90.5 13.0 %collective-permute-start.9 = (f32[108,8,128]{2,1,0:T(8,128)}, f32[108,8,128]{2,1,0:T(8,128)S(1)}, u32[]{:S(2)}, u32[]{:S(2)}) collective-permute-start(f32[108,8,128]{2,1,0:T(8,128)} %get-tuple-element.56), channel_id=1, source_target_pairs={{0,3},{1,0},{2,1},{3,2},{4,7},{5,4},{6,5},{7,6},{8,11},{9,8},{10,9... | collective-permute-start | bytes 1327112 | tf_op jit(solution)/shard_map/ppermute | solution.py:650
  103.5 0.0 collective-permute-done.5.refs_3_
  103.5 0.7 copy-done.11
  104.2 0.0 collective-permute-start.8
  104.2 0.0 collective-permute-done.4.refs_2_
  104.2 0.3 collective-permute-start.7
  104.5 0.0 collective-permute-done.10
  104.5 0.0 collective-permute-done.11
  104.5 0.0 copy-start.6
  104.5 0.8 copy-done.5
  105.3 0.2 copy-done.6
  105.5 12.8 %front.7 = (f32[72,8,128]{2,1,0:T(8,128)}, f32[72,8,128]{2,1,0:T(8,128)}, f32[72,8,128]{2,1,0:T(8,128)}, f32[72,8,128]{2,1,0:T(8,128)}) custom-call(f32[36]{0:T(128)} %constant.21.clone.tab_ref, f32[2,36]{1,0:T(2,128)} %constant.24.clone.dir_ref, s32[1]{0:T(128)} %bitcast.2.pos_ref, s32[4,32,128]{2,1,0:T(8,128)} %bitcast.37, f32[32,128]{1,0:T(8,128)} %bitcast.43, ...), custom_call_target="tpu_custom_call" | custom-call | bytes 44000000 | tf_op jit(solution)/shard_map/front/pallas_call | solution.py:440
  118.3 0.0 collective-permute-done.9.refs_8_
  118.3 0.0 copy-start.7
  118.4 3.0 %collective-permute-start.14 = (f32[72,8,128]{2,1,0:T(8,128)}, f32[72,8,128]{2,1,0:T(8,128)S(1)}, u32[]{:S(2)}, u32[]{:S(2)}) collective-permute-start(f32[72,8,128]{2,1,0:T(8,128)} %get-tuple-element.66), channel_id=1, source_target_pairs={{0,3},{1,0},{2,1},{3,2},{4,7},{5,4},{6,5},{7,6},{8,11},{9,8},{10,9... | collective-permute-start | bytes 884744 | tf_op jit(solution)/shard_map/ppermute | solution.py:650
  121.4 25.3 %collective-permute-done.8.refs_7_ = f32[108,8,128]{2,1,0:T(8,128)S(1)} collective-permute-done((f32[108,8,128]{2,1,0:T(8,128)}, f32[108,8,128]{2,1,0:T(8,128)S(1)}, u32[]{:S(2)}, u32[]{:S(2)}) %collective-permute-start.8) | collective-permute-done | bytes 442400 | tf_op jit(solution)/shard_map/ppermute | solution.py:650
  146.7 0.0 collective-permute-start.13
  146.7 0.0 collective-permute-done.7.refs_6_
  146.7 11.0 %collective-permute-start.12 = (f32[72,8,128]{2,1,0:T(8,128)}, f32[72,8,128]{2,1,0:T(8,128)S(1)}, u32[]{:S(2)}, u32[]{:S(2)}) collective-permute-start(f32[72,8,128]{2,1,0:T(8,128)} %get-tuple-element.62), channel_id=1, source_target_pairs={{0,1},{1,2},{2,3},{3,0},{4,5},{5,6},{6,7},{7,4},{8,9},{9,10},{10,1... | collective-permute-start | bytes 884744 | tf_op jit(solution)/shard_map/ppermute | solution.py:650
  157.7 0.6 copy.22
  158.3 0.3 copy.15
  158.5 0.9 reshape.42.spot_ref
  159.5 0.3 copy.16
  159.7 0.9 reshape.43.wts_ref
  160.7 1.3 dynamic-slice_bitcast_fusion.1.mask_ref
  162.0 0.0 collective-permute-done.14.refs_12_
  162.0 10.0 %collective-permute-done.13.refs_11_ = f32[72,8,128]{2,1,0:T(8,128)S(1)} collective-permute-done((f32[72,8,128]{2,1,0:T(8,128)}, f32[72,8,128]{2,1,0:T(8,128)S(1)}, u32[]{:S(2)}, u32[]{:S(2)}) %collective-permute-start.13) | collective-permute-done | bytes 294944 | tf_op jit(solution)/shard_map/ppermute | solution.py:650
  172.0 0.0 collective-permute-done.12.refs_10_
  172.0 0.7 copy-done.13
  172.7 0.1 copy-done.14
  172.8 23.2 %tail.1 = f32[1296,1024]{1,0:T(8,128)} custom-call(s32[5184]{0:T(1024)} %reshape.42.spot_ref, f32[2592]{0:T(1024)} %reshape.43.wts_ref, f32[3,36]{1,0:T(4,128)} %constant.22.clone.ftab_ref, f32[1296]{0:T(1024)} %constant.23.clone.frs_ref, f32[2,36]{1,0:T(2,128)} %constant.24.clone.dir_ref, s32[1]{0:T(128)} %bitcast.2.pos_ref, f32[2,8,128]{2,1,0:T(8,128)} %bitcast.58, ...), custom_call_target="tpu_custom_call" | custom-call | bytes 70000000 | tf_op jit(solution)/shard_map/tail/pallas_call | solution.py:555
  (20 shorter events, 0.0 us)
Async XLA Ops:
  0.0 157.7 %copy-start = (f32[2,4096]{1,0:T(2,128)S(1)}, f32[2,4096]{1,0:T(2,128)}, u32[]{:S(2)}) copy-start(f32[2,4096]{1,0:T(2,128)} %param.15) | copy-start | bytes 98308
  3.2 13.4 %collective-permute-start = (f32[2,592,128]{2,1,0:T(8,128)}, f32[2,592,128]{2,1,0:T(8,128)S(1)}, u32[]{:S(2)}, u32[]{:S(2)}) collective-permute-start(f32[2,592,128]{2,1,0:T(8,128)} %get-tuple-element.36), channel_id=1, source_target_pairs={{0,4},{4,8},{8,12},{1,5},{5,9},{9,13},{2,6},{6,10},{10,14},{3,7},{... | collective-permute-start | bytes 1818632 | tf_op jit(solution)/shard_map/ppermute | solution.py:611
  7.7 16.2 %copy-start.15 = (s32[4,4096]{1,0:T(4,128)S(1)}, s32[4,4096]{1,0:T(4,128)}, u32[]{:S(2)}) copy-start(s32[4,4096]{1,0:T(4,128)} %param.17) | copy-start | bytes 196612
  7.7 11.7 %collective-permute-start.1 = (f32[2,592,128]{2,1,0:T(8,128)}, f32[2,592,128]{2,1,0:T(8,128)S(1)}, u32[]{:S(2)}, u32[]{:S(2)}) collective-permute-start(f32[2,592,128]{2,1,0:T(8,128)} %get-tuple-element.37), channel_id=1, source_target_pairs={{4,0},{8,4},{12,8},{5,1},{9,5},{13,9},{6,2},{10,6},{14,10},{7,3},{... | collective-permute-start | bytes 1818632 | tf_op jit(solution)/shard_map/ppermute | solution.py:611
  16.6 8.0 %copy-start.3 = (f32[2,592,128]{2,1,0:T(8,128)}, f32[2,592,128]{2,1,0:T(8,128)S(1)}, u32[]{:S(2)}) copy-start(f32[2,592,128]{2,1,0:T(8,128)S(1)} %collective-permute-done.hs_ref) | copy-start | bytes 1818628
  19.4 5.1 %copy-start.4 = (f32[2,592,128]{2,1,0:T(8,128)}, f32[2,592,128]{2,1,0:T(8,128)S(1)}, u32[]{:S(2)}) copy-start(f32[2,592,128]{2,1,0:T(8,128)S(1)} %collective-permute-done.1.hn_ref) | copy-start | bytes 1818628
  19.4 25.5 %collective-permute-start.2 = (f32[7,592,128]{2,1,0:T(8,128)}, f32[7,592,128]{2,1,0:T(8,128)S(1)}, u32[]{:S(2)}, u32[]{:S(2)}) collective-permute-start(f32[7,592,128]{2,1,0:T(8,128)} %get-tuple-element.42), channel_id=1, source_target_pairs={{0,4},{4,8},{8,12},{1,5},{5,9},{9,13},{2,6},{6,10},{10,14},{3,7},{... | collective-permute-start | bytes 6365192 | tf_op jit(solution)/shard_map/ppermute | solution.py:611
  21.4 28.1 %collective-permute-start.3 = (f32[7,592,128]{2,1,0:T(8,128)}, f32[7,592,128]{2,1,0:T(8,128)}, u32[]{:S(2)}, u32[]{:S(2)}) collective-permute-start(f32[7,592,128]{2,1,0:T(8,128)} %get-tuple-element.43), channel_id=1, source_target_pairs={{4,0},{8,4},{12,8},{5,1},{9,5},{13,9},{6,2},{10,6},{14,10},{7,3},{... | collective-permute-start | bytes 6365192 | tf_op jit(solution)/shard_map/ppermute | solution.py:611
  37.1 34.4 %all-to-all-start = ((f32[4,72,8,128]{3,2,1,0:T(8,128)}), f32[4,72,8,128]{3,2,1,0:T(8,128)S(1)}, u32[]{:S(2)}, u32[]{:S(2)}) async-start(f32[4,72,8,128]{3,2,1,0:T(8,128)} %front.4), calls=%async_computation | async-start | bytes 2359296 | tf_op jit(solution)/shard_map/all_to_all | solution.py:643
  44.9 4.6 %copy-start.1 = (f32[7,592,128]{2,1,0:T(8,128)}, f32[7,592,128]{2,1,0:T(8,128)S(1)}, u32[]{:S(2)}) copy-start(f32[7,592,128]{2,1,0:T(8,128)S(1)} %collective-permute-done.2.hs_ref) | copy-start | bytes 6365188
  62.2 27.5 %collective-permute-start.6 = (f32[72,8,128]{2,1,0:T(8,128)}, f32[72,8,128]{2,1,0:T(8,128)S(1)}, u32[]{:S(2)}, u32[]{:S(2)}) collective-permute-start(f32[72,8,128]{2,1,0:T(8,128)} %get-tuple-element.48), channel_id=1, source_target_pairs={{0,3},{1,0},{2,1},{3,2},{4,7},{5,4},{6,5},{7,6},{8,11},{9,8},{10,9... | collective-permute-start | bytes 884744 | tf_op jit(solution)/shard_map/ppermute | solution.py:650
  65.6 37.9 %collective-permute-start.5 = (f32[72,8,128]{2,1,0:T(8,128)}, f32[72,8,128]{2,1,0:T(8,128)S(1)}, u32[]{:S(2)}, u32[]{:S(2)}) collective-permute-start(f32[72,8,128]{2,1,0:T(8,128)} %get-tuple-element.47), channel_id=1, source_target_pairs={{0,2},{1,3},{2,0},{3,1},{4,6},{5,7},{6,4},{7,5},{8,10},{9,11},{10,... | collective-permute-start | bytes 884744 | tf_op jit(solution)/shard_map/ppermute | solution.py:650
  65.6 38.6 %collective-permute-start.4 = (f32[72,8,128]{2,1,0:T(8,128)}, f32[72,8,128]{2,1,0:T(8,128)}, u32[]{:S(2)}, u32[]{:S(2)}) collective-permute-start(f32[72,8,128]{2,1,0:T(8,128)} %get-tuple-element.46), channel_id=1, source_target_pairs={{0,1},{1,2},{2,3},{3,0},{4,5},{5,6},{6,7},{7,4},{8,9},{9,10},{10,1... | collective-permute-start | bytes 884744 | tf_op jit(solution)/shard_map/ppermute | solution.py:650
  66.1 38.4 %collective-permute-start.10 = (f32[1152,128]{1,0:T(8,128)}, f32[1152,128]{1,0:T(8,128)S(1)}, u32[]{:S(2)}, u32[]{:S(2)}) collective-permute-start(f32[1152,128]{1,0:T(8,128)} %get-tuple-element.58), channel_id=1, source_target_pairs={{0,1},{1,2},{2,3},{4,5},{5,6},{6,7},{8,9},{9,10},{10,11},{12,13},{... | collective-permute-start | bytes 1769480 | tf_op jit(solution)/shard_map/ppermute | solution.py:611
  70.2 34.3 %collective-permute-start.11 = (f32[1152,128]{1,0:T(8,128)}, f32[1152,128]{1,0:T(8,128)S(1)}, u32[]{:S(2)}, u32[]{:S(2)}) collective-permute-start(f32[1152,128]{1,0:T(8,128)} %get-tuple-element.59), channel_id=1, source_target_pairs={{1,0},{2,1},{3,2},{5,4},{6,5},{7,6},{9,8},{10,9},{11,10},{13,12},{... | collective-permute-start | bytes 1769480 | tf_op jit(solution)/shard_map/ppermute | solution.py:611
  71.5 18.2 %copy-start.2 = (f32[4,72,8,128]{3,2,1,0:T(8,128)}, f32[4,72,8,128]{3,2,1,0:T(8,128)S(1)}, u32[]{:S(2)}) copy-start(f32[4,72,8,128]{3,2,1,0:T(8,128)S(1)} %all-to-all-done.refs_0_) | copy-start | bytes 3538948
  89.7 0.7 copy-start.10
  90.5 27.9 %collective-permute-start.9 = (f32[108,8,128]{2,1,0:T(8,128)}, f32[108,8,128]{2,1,0:T(8,128)S(1)}, u32[]{:S(2)}, u32[]{:S(2)}) collective-permute-start(f32[108,8,128]{2,1,0:T(8,128)} %get-tuple-element.56), channel_id=1, source_target_pairs={{0,3},{1,0},{2,1},{3,2},{4,7},{5,4},{6,5},{7,6},{8,11},{9,8},{10,9... | collective-permute-start | bytes 1327112 | tf_op jit(solution)/shard_map/ppermute | solution.py:650
  103.5 0.7 copy-start.11
  104.2 42.5 %collective-permute-start.8 = (f32[108,8,128]{2,1,0:T(8,128)}, f32[108,8,128]{2,1,0:T(8,128)S(1)}, u32[]{:S(2)}, u32[]{:S(2)}) collective-permute-start(f32[108,8,128]{2,1,0:T(8,128)} %get-tuple-element.54), channel_id=1, source_target_pairs={{0,2},{1,3},{2,0},{3,1},{4,6},{5,7},{6,4},{7,5},{8,10},{9,11},{10,... | collective-permute-start | bytes 1327112 | tf_op jit(solution)/shard_map/ppermute | solution.py:650
  104.2 42.5 %collective-permute-start.7 = (f32[108,8,128]{2,1,0:T(8,128)}, f32[108,8,128]{2,1,0:T(8,128)S(1)}, u32[]{:S(2)}, u32[]{:S(2)}) collective-permute-start(f32[108,8,128]{2,1,0:T(8,128)} %get-tuple-element.52), channel_id=1, source_target_pairs={{0,1},{1,2},{2,3},{3,0},{4,5},{5,6},{6,7},{7,4},{8,9},{9,10},{10,1... | collective-permute-start | bytes 1327112 | tf_op jit(solution)/shard_map/ppermute | solution.py:650
  104.5 0.8 copy-start.5
  104.5 1.0 copy-start.6
  105.5 52.8 %copy-start.16 = (s32[4,1296]{1,0:T(4,128)S(1)}, s32[4,1296]{1,0:T(4,128)}, u32[]{:S(2)}) copy-start(s32[4,1296]{1,0:T(4,128)} %param.22) | copy-start | bytes 62212
  105.5 54.0 %copy-start.17 = (f32[2,1296]{1,0:T(2,128)S(1)}, f32[2,1296]{1,0:T(2,128)}, u32[]{:S(2)}) copy-start(f32[2,1296]{1,0:T(2,128)} %param.23) | copy-start | bytes 31108
  118.3 53.6 %copy-start.7 = (f32[108,8,128]{2,1,0:T(8,128)}, f32[108,8,128]{2,1,0:T(8,128)S(1)}, u32[]{:S(2)}) copy-start(f32[108,8,128]{2,1,0:T(8,128)S(1)} %collective-permute-done.9.refs_8_) | copy-start | bytes 1327108
  118.4 43.6 %collective-permute-start.14 = (f32[72,8,128]{2,1,0:T(8,128)}, f32[72,8,128]{2,1,0:T(8,128)S(1)}, u32[]{:S(2)}, u32[]{:S(2)}) collective-permute-start(f32[72,8,128]{2,1,0:T(8,128)} %get-tuple-element.66), channel_id=1, source_target_pairs={{0,3},{1,0},{2,1},{3,2},{4,7},{5,4},{6,5},{7,6},{8,11},{9,8},{10,9... | collective-permute-start | bytes 884744 | tf_op jit(solution)/shard_map/ppermute | solution.py:650
  146.7 25.3 %copy-start.8 = (f32[108,8,128]{2,1,0:T(8,128)}, f32[108,8,128]{2,1,0:T(8,128)S(1)}, u32[]{:S(2)}) copy-start(f32[108,8,128]{2,1,0:T(8,128)S(1)} %collective-permute-done.8.refs_7_) | copy-start | bytes 1327108
  146.7 25.3 %collective-permute-start.13 = (f32[72,8,128]{2,1,0:T(8,128)}, f32[72,8,128]{2,1,0:T(8,128)S(1)}, u32[]{:S(2)}, u32[]{:S(2)}) collective-permute-start(f32[72,8,128]{2,1,0:T(8,128)} %get-tuple-element.64), channel_id=1, source_target_pairs={{0,2},{1,3},{2,0},{3,1},{4,6},{5,7},{6,4},{7,5},{8,10},{9,11},{10,... | collective-permute-start | bytes 884744 | tf_op jit(solution)/shard_map/ppermute | solution.py:650
  146.7 25.3 %copy-start.9 = (f32[108,8,128]{2,1,0:T(8,128)}, f32[108,8,128]{2,1,0:T(8,128)S(1)}, u32[]{:S(2)}) copy-start(f32[108,8,128]{2,1,0:T(8,128)S(1)} %collective-permute-done.7.refs_6_) | copy-start | bytes 1327108
  146.7 25.3 %collective-permute-start.12 = (f32[72,8,128]{2,1,0:T(8,128)}, f32[72,8,128]{2,1,0:T(8,128)S(1)}, u32[]{:S(2)}, u32[]{:S(2)}) collective-permute-start(f32[72,8,128]{2,1,0:T(8,128)} %get-tuple-element.62), channel_id=1, source_target_pairs={{0,1},{1,2},{2,3},{3,0},{4,5},{5,6},{6,7},{7,4},{8,9},{9,10},{10,1... | collective-permute-start | bytes 884744 | tf_op jit(solution)/shard_map/ppermute | solution.py:650
  162.0 10.0 %copy-start.12 = (f32[72,8,128]{2,1,0:T(8,128)}, f32[72,8,128]{2,1,0:T(8,128)S(1)}, u32[]{:S(2)}) copy-start(f32[72,8,128]{2,1,0:T(8,128)S(1)} %collective-permute-done.14.refs_12_) | copy-start | bytes 884740
  171.9 0.7 copy-start.13
  172.0 0.8 copy-start.14
where the time goes:
time: 197 us; the launch traced here: 196 us
  Pallas kernels  89.4 us (45%)
  starting transfers between devices  52.1 us (26%)
  waiting for transfers between devices  45.9 us (23%)
  local copies, waits for them, and re-layouts  8.15 us (4%)
    pallas_call x4, Pallas kernels, front(): pl.pallas_call(functools.partial(front_kernel, tiles, shares, nloc, kmin,...  56.4 us
    ppermute x9, waiting for transfers between devices, fast_on_device(): lax.ppermute(rows, 'bin', [(i, (i + d) % shares) for i in range(shares)])  35.3 us
    ppermute x9, starting transfers between devices, fast_on_device(): lax.ppermute(rows, 'bin', [(i, (i + d) % shares) for i in range(shares)])  31.1 us
    pallas_call x1, Pallas kernels, tail(): pl.pallas_call(functools.partial(tail_kernel, nfreq, bins_dev, plan), out...  23.2 us
    ppermute x6, starting transfers between devices, line(): return lax.ppermute(array, axis, pairs)  16.4 us
    ppermute x6, waiting for transfers between devices, line(): return lax.ppermute(array, axis, pairs)  10.6 us
    pallas_call x2, Pallas kernels, prep(): pl.pallas_call(functools.partial(prep_kernel, points, bins, blocks, group...  9.91 us
    all_to_all x1, starting transfers between devices, fast_on_device(): lax.all_to_all(blocks[0], 'bin', split_axis=0, concat_axis=0, tiled=True)  4.59 us
  transfers between devices with their start and end apart: 16, of which 5 were waited for; matrix products, arithmetic and copies ran while one was open for 3% of the time, Pallas kernels for 32%

commit v1 on v0

--- a/solution.py
+++ b/solution.py
@@ -640,7 +640,8 @@
         earlier = sum(halos, ()) if c == 0 else arrived[0] if c == 1 else []
         order, *_ = lax.optimization_barrier((pos, blocks[0], *earlier))
         if joined:
-            arrived.append([lax.all_to_all(blocks[0], "bin", split_axis=0, concat_axis=0, tiled=True)])
+            blocks, *_ = lax.optimization_barrier((blocks[0], low_in, high_in))
+            arrived.append([lax.all_to_all(blocks, "bin", split_axis=0, concat_axis=0, tiled=True)])
             continue
         here = [blocks[0]]
         for d in range(1, shares):

time: 197 us -> 197 us (level); the launches traced: 196 us -> 193 us
  waiting for transfers between devices: 45.9 us -> 43.5 us
    all_to_all x1, waiting for transfers between devices: 0.01 us -> 10.2 us  [fast_on_device(): lax.all_to_all(blocks, 'bin', split_axis=0, concat_axis=0, tiled=True)]
    ppermute x9, waiting for transfers between devices: 35.3 us -> 27.3 us  [fast_on_device(): lax.ppermute(rows, 'bin', [(i, (i + d) % shares) for i in range(shares)])]
    ppermute x6, waiting for transfers between devices: 10.6 us -> 6.04 us  [line(): return lax.ppermute(array, axis, pairs)]
    unnamed x39 -> x37, local copies, waits for them, and re-layouts: 4.48 us -> 3.8 us
  transfers between devices with their start and end apart: 16 -> 16, of which waited for: 5 -> 6; matrix products, arithmetic and copies ran while one was open for 3% -> 3% of each run, Pallas kernels for 32% -> 33%
where the time goes in v1:
time: 197 us; the launch traced here: 193 us
  Pallas kernels  89.6 us (45%)
  starting transfers between devices  52.5 us (27%)
  waiting for transfers between devices  43.5 us (22%)
  local copies, waits for them, and re-layouts  7.48 us (4%)
    pallas_call x4, Pallas kernels, front(): pl.pallas_call(functools.partial(front_kernel, tiles, shares, nloc, kmin,...  56.5 us
    ppermute x9, starting transfers between devices, fast_on_device(): lax.ppermute(rows, 'bin', [(i, (i + d) % shares) for i in range(shares)])  32.6 us
    ppermute x9, waiting for transfers between devices, fast_on_device(): lax.ppermute(rows, 'bin', [(i, (i + d) % shares) for i in range(shares)])  27.3 us
    pallas_call x1, Pallas kernels, tail(): pl.pallas_call(functools.partial(tail_kernel, nfreq, bins_dev, plan), out...  23.2 us
    ppermute x6, starting transfers between devices, line(): return lax.ppermute(array, axis, pairs)  16.3 us
    all_to_all x1, waiting for transfers between devices, fast_on_device(): lax.all_to_all(blocks, 'bin', split_axis=0, concat_axis=0, tiled=True)  10.2 us
    pallas_call x2, Pallas kernels, prep(): pl.pallas_call(functools.partial(prep_kernel, points, bins, blocks, group...  9.91 us
    ppermute x6, waiting for transfers between devices, line(): return lax.ppermute(array, axis, pairs)  6.04 us
  transfers between devices with their start and end apart: 16, of which 6 were waited for; matrix products, arithmetic and copies ran while one was open for 3% of the time, Pallas kernels for 33%

profile of v1, /device:TPU:1, one launch (start us, length us, event | category | flops | bytes accessed | tf_op | source)
XLA Modules:
  0.0 193.5 jit_solution(6399691062816306457)
XLA Ops:
  0.0 0.0 copy-start
  0.0 3.1 %prep.2 = (f32[2,592,128]{2,1,0:T(8,128)}, f32[2,592,128]{2,1,0:T(8,128)}) custom-call(f32[324,4096]{1,0:T(8,128)} %spec_hbm.2, s32[1,4096]{1,0:T(1,128)} %bitcast.54), custom_call_target="tpu_custom_call" | custom-call | bytes 6000000 | tf_op jit(solution)/shard_map/prep/pallas_call | solution.py:300
  3.2 4.5 %collective-permute-start = (f32[2,592,128]{2,1,0:T(8,128)}, f32[2,592,128]{2,1,0:T(8,128)S(1)}, u32[]{:S(2)}, u32[]{:S(2)}) collective-permute-start(f32[2,592,128]{2,1,0:T(8,128)} %get-tuple-element.37), channel_id=1, source_target_pairs={{0,4},{4,8},{8,12},{1,5},{5,9},{9,13},{2,6},{6,10},{10,14},{3,7},{... | collective-permute-start | bytes 1818632 | tf_op jit(solution)/shard_map/ppermute | solution.py:611
  7.7 0.0 copy-start.14
  7.7 2.1 %collective-permute-start.1 = (f32[2,592,128]{2,1,0:T(8,128)}, f32[2,592,128]{2,1,0:T(8,128)S(1)}, u32[]{:S(2)}, u32[]{:S(2)}) collective-permute-start(f32[2,592,128]{2,1,0:T(8,128)} %get-tuple-element.38), channel_id=1, source_target_pairs={{4,0},{8,4},{12,8},{5,1},{9,5},{13,9},{6,2},{10,6},{14,10},{7,3},{... | collective-permute-start | bytes 1818632 | tf_op jit(solution)/shard_map/ppermute | solution.py:611
  9.8 6.8 %prep.3 = (f32[7,592,128]{2,1,0:T(8,128)}, f32[7,592,128]{2,1,0:T(8,128)}, f32[10368,128]{1,0:T(8,128)}, f32[1152,128]{1,0:T(8,128)}, f32[1152,128]{1,0:T(8,128)}) custom-call(f32[324,4096]{1,0:T(8,128)} %spec_hbm.2, s32[1,4096]{1,0:T(1,128)} %bitcast.55), custom_call_target="tpu_custom_call" | custom-call | bytes 27000000 | tf_op jit(solution)/shard_map/prep/pallas_call | solution.py:300
  16.5 0.0 collective-permute-done.hs_ref
  16.6 0.0 copy-start.3
  16.6 2.9 %collective-permute-done.1.hn_ref = f32[2,592,128]{2,1,0:T(8,128)S(1)} collective-permute-done((f32[2,592,128]{2,1,0:T(8,128)}, f32[2,592,128]{2,1,0:T(8,128)S(1)}, u32[]{:S(2)}, u32[]{:S(2)}) %collective-permute-start.1) | collective-permute-done | bytes 606240 | tf_op jit(solution)/shard_map/ppermute | solution.py:611
  19.4 1.9 collective-permute-start.4
  21.4 2.5 %collective-permute-start.5 = (f32[7,592,128]{2,1,0:T(8,128)}, f32[7,592,128]{2,1,0:T(8,128)}, u32[]{:S(2)}, u32[]{:S(2)}) collective-permute-start(f32[7,592,128]{2,1,0:T(8,128)} %get-tuple-element.47), channel_id=1, source_target_pairs={{4,0},{8,4},{12,8},{5,1},{9,5},{13,9},{6,2},{10,6},{14,10},{7,3},{... | collective-permute-start | bytes 6365192 | tf_op jit(solution)/shard_map/ppermute | solution.py:611
  23.9 4.0 %collective-permute-start.2 = (f32[1152,128]{1,0:T(8,128)}, f32[1152,128]{1,0:T(8,128)}, u32[]{:S(2)}, u32[]{:S(2)}) collective-permute-start(f32[1152,128]{1,0:T(8,128)} %get-tuple-element.41), channel_id=1, source_target_pairs={{0,1},{1,2},{2,3},{4,5},{5,6},{6,7},{8,9},{9,10},{10,11},{12,13},{... | collective-permute-start | bytes 1769480 | tf_op jit(solution)/shard_map/ppermute | solution.py:611
  27.9 1.3 collective-permute-start.3
  29.2 0.0 copy-done.14
  29.2 0.6 copy.21
  29.9 0.0 copy-done.3
  29.9 0.0 copy-done.4
  29.9 12.7 %front.4 = f32[4,72,8,128]{3,2,1,0:T(8,128)} custom-call(f32[36]{0:T(128)} %constant.21.clone.tab_ref, f32[2,36]{1,0:T(2,128)} %constant.24.clone.dir_ref, s32[1]{0:T(128)} %bitcast.2.pos_ref, s32[4,32,128]{2,1,0:T(8,128)} %bitcast.34, f32[32,128]{1,0:T(8,128)} %bitcast.38, f32[32,128]{1,0:T(8,128)} %bitcast.42, f32[32,128]{1,0:T(8,128)} %bitcast.46, ...), custom_call_target="tpu_custom_call" | custom-call | bytes 44000000 | tf_op jit(solution)/shard_map/front/pallas_call | solution.py:440
  42.6 0.0 collective-permute-done.2
  42.6 2.8 %collective-permute-done.3 = f32[1152,128]{1,0:T(8,128)} collective-permute-done((f32[1152,128]{1,0:T(8,128)}, f32[1152,128]{1,0:T(8,128)}, u32[]{:S(2)}, u32[]{:S(2)}) %collective-permute-start.3) | collective-permute-done | bytes 589856 | tf_op jit(solution)/shard_map/ppermute | solution.py:611
  45.3 3.5 %all-to-all-start = ((f32[4,72,8,128]{3,2,1,0:T(8,128)}), f32[4,72,8,128]{3,2,1,0:T(8,128)S(1)}, u32[]{:S(2)}, u32[]{:S(2)}) async-start(f32[4,72,8,128]{3,2,1,0:T(8,128)} %front.4), calls=%async_computation | async-start | bytes 2359296 | tf_op jit(solution)/shard_map/all_to_all | solution.py:644
  48.9 0.0 collective-permute-done.4.hs_ref
  48.9 0.0 copy-start.1
  48.9 0.4 collective-permute-done.5.hn_ref
  49.3 0.9 copy-done.1
  50.2 12.7 %front.5 = (f32[72,8,128]{2,1,0:T(8,128)}, f32[72,8,128]{2,1,0:T(8,128)}, f32[72,8,128]{2,1,0:T(8,128)}, f32[72,8,128]{2,1,0:T(8,128)}) custom-call(f32[36]{0:T(128)} %constant.21.clone.tab_ref, f32[2,36]{1,0:T(2,128)} %constant.24.clone.dir_ref, s32[1]{0:T(128)} %bitcast.2.pos_ref, s32[4,32,128]{2,1,0:T(8,128)} %bitcast.35, f32[32,128]{1,0:T(8,128)} %bitcast.39, ...), custom_call_target="tpu_custom_call" | custom-call | bytes 44000000 | tf_op jit(solution)/shard_map/front/pallas_call | solution.py:440
  63.0 3.3 %collective-permute-start.8 = (f32[72,8,128]{2,1,0:T(8,128)}, f32[72,8,128]{2,1,0:T(8,128)S(1)}, u32[]{:S(2)}, u32[]{:S(2)}) collective-permute-start(f32[72,8,128]{2,1,0:T(8,128)} %get-tuple-element.52), channel_id=1, source_target_pairs={{0,3},{1,0},{2,1},{3,2},{4,7},{5,4},{6,5},{7,6},{8,11},{9,8},{10,9... | collective-permute-start | bytes 884744 | tf_op jit(solution)/shard_map/ppermute | solution.py:651
  66.2 0.0 collective-permute-start.7
  66.2 0.5 collective-permute-start.6
  66.8 10.2 %all-to-all-done.refs_0_ = f32[4,72,8,128]{3,2,1,0:T(8,128)S(1)} async-done(((f32[4,72,8,128]{3,2,1,0:T(8,128)}), f32[4,72,8,128]{3,2,1,0:T(8,128)S(1)}, u32[]{:S(2)}, u32[]{:S(2)}) %all-to-all-start) | async-done | bytes 1179680 | tf_op jit(solution)/shard_map/all_to_all | solution.py:644
  77.0 18.2 %front.6 = (f32[108,8,128]{2,1,0:T(8,128)}, f32[108,8,128]{2,1,0:T(8,128)}, f32[108,8,128]{2,1,0:T(8,128)}, f32[108,8,128]{2,1,0:T(8,128)}) custom-call(f32[36]{0:T(128)} %constant.21.clone.tab_ref, f32[2,36]{1,0:T(2,128)} %constant.24.clone.dir_ref, s32[1]{0:T(128)} %bitcast.2.pos_ref, s32[4,32,128]{2,1,0:T(8,128)} %bitcast.36, f32[32,128]{1,0:T(8,128)} %bitcast.40, ...), custom_call_target="tpu_custom_call" | custom-call | bytes 66000000 | tf_op jit(solution)/shard_map/front/pallas_call | solution.py:440
  95.2 0.0 copy-done.2
  95.2 0.0 collective-permute-done.8.refs_4_
  95.2 0.0 copy-start.8
  95.2 13.9 %collective-permute-start.11 = (f32[108,8,128]{2,1,0:T(8,128)}, f32[108,8,128]{2,1,0:T(8,128)S(1)}, u32[]{:S(2)}, u32[]{:S(2)}) collective-permute-start(f32[108,8,128]{2,1,0:T(8,128)} %get-tuple-element.60), channel_id=1, source_target_pairs={{0,3},{1,0},{2,1},{3,2},{4,7},{5,4},{6,5},{7,6},{8,11},{9,8},{10,9... | collective-permute-start | bytes 1327112 | tf_op jit(solution)/shard_map/ppermute | solution.py:651
  109.1 0.0 collective-permute-done.7.refs_3_
  109.1 0.0 collective-permute-start.10
  109.1 0.0 collective-permute-done.6.refs_2_
  109.2 0.0 copy-start.10
  109.2 0.8 copy-done.10
  110.0 0.3 collective-permute-start.9
  110.2 12.9 %front.7 = (f32[72,8,128]{2,1,0:T(8,128)}, f32[72,8,128]{2,1,0:T(8,128)}, f32[72,8,128]{2,1,0:T(8,128)}, f32[72,8,128]{2,1,0:T(8,128)}) custom-call(f32[36]{0:T(128)} %constant.21.clone.tab_ref, f32[2,36]{1,0:T(2,128)} %constant.24.clone.dir_ref, s32[1]{0:T(128)} %bitcast.2.pos_ref, s32[4,32,128]{2,1,0:T(8,128)} %bitcast.37, f32[32,128]{1,0:T(8,128)} %bitcast.41, ...), custom_call_target="tpu_custom_call" | custom-call | bytes 44000000 | tf_op jit(solution)/shard_map/front/pallas_call | solution.py:440
  123.2 0.0 copy-done.8
  123.2 0.0 copy-done.9
  123.2 0.0 collective-permute-done.11.refs_8_
  123.2 0.0 copy-start.5
  123.2 3.0 %collective-permute-start.14 = (f32[72,8,128]{2,1,0:T(8,128)}, f32[72,8,128]{2,1,0:T(8,128)S(1)}, u32[]{:S(2)}, u32[]{:S(2)}) collective-permute-start(f32[72,8,128]{2,1,0:T(8,128)} %get-tuple-element.68), channel_id=1, source_target_pairs={{0,3},{1,0},{2,1},{3,2},{4,7},{5,4},{6,5},{7,6},{8,11},{9,8},{10,9... | collective-permute-start | bytes 884744 | tf_op jit(solution)/shard_map/ppermute | solution.py:651
  126.2 19.0 %collective-permute-done.10.refs_7_ = f32[108,8,128]{2,1,0:T(8,128)S(1)} collective-permute-done((f32[108,8,128]{2,1,0:T(8,128)}, f32[108,8,128]{2,1,0:T(8,128)S(1)}, u32[]{:S(2)}, u32[]{:S(2)}) %collective-permute-start.10) | collective-permute-done | bytes 442400 | tf_op jit(solution)/shard_map/ppermute | solution.py:651
  145.2 0.0 collective-permute-start.13
  145.2 0.0 collective-permute-done.9.refs_6_
  145.2 11.6 %collective-permute-start.12 = (f32[72,8,128]{2,1,0:T(8,128)}, f32[72,8,128]{2,1,0:T(8,128)S(1)}, u32[]{:S(2)}, u32[]{:S(2)}) collective-permute-start(f32[72,8,128]{2,1,0:T(8,128)} %get-tuple-element.64), channel_id=1, source_target_pairs={{0,1},{1,2},{2,3},{3,0},{4,5},{5,6},{6,7},{7,4},{8,9},{9,10},{10,1... | collective-permute-start | bytes 884744 | tf_op jit(solution)/shard_map/ppermute | solution.py:651
  156.8 0.0 copy-done
  156.8 0.6 copy.22
  157.4 0.3 copy.15
  157.7 1.0 reshape.42.spot_ref
  158.7 0.3 copy.16
  158.9 0.9 reshape.43.wts_ref
  159.8 1.3 dynamic-slice_bitcast_fusion.1.mask_ref
  161.1 0.0 collective-permute-done.14.refs_12_
  161.1 8.3 %collective-permute-done.13.refs_11_ = f32[72,8,128]{2,1,0:T(8,128)S(1)} collective-permute-done((f32[72,8,128]{2,1,0:T(8,128)}, f32[72,8,128]{2,1,0:T(8,128)S(1)}, u32[]{:S(2)}, u32[]{:S(2)}) %collective-permute-start.13) | collective-permute-done | bytes 294944 | tf_op jit(solution)/shard_map/ppermute | solution.py:651
  169.4 0.0 collective-permute-done.12.refs_10_
  169.5 0.7 copy-done.12
  170.2 0.1 copy-done.13
  170.3 23.2 %tail.1 = f32[1296,1024]{1,0:T(8,128)} custom-call(s32[5184]{0:T(1024)} %reshape.42.spot_ref, f32[2592]{0:T(1024)} %reshape.43.wts_ref, f32[3,36]{1,0:T(4,128)} %constant.22.clone.ftab_ref, f32[1296]{0:T(1024)} %constant.23.clone.frs_ref, f32[2,36]{1,0:T(2,128)} %constant.24.clone.dir_ref, s32[1]{0:T(128)} %bitcast.2.pos_ref, f32[2,8,128]{2,1,0:T(8,128)} %bitcast.56, ...), custom_call_target="tpu_custom_call" | custom-call | bytes 70000000 | tf_op jit(solution)/shard_map/tail/pallas_call | solution.py:555
  (18 shorter events, 0.0 us)
Async XLA Ops:
  0.0 156.8 %copy-start = (f32[2,4096]{1,0:T(2,128)S(1)}, f32[2,4096]{1,0:T(2,128)}, u32[]{:S(2)}) copy-start(f32[2,4096]{1,0:T(2,128)} %param.15) | copy-start | bytes 98308
  3.2 13.4 %collective-permute-start = (f32[2,592,128]{2,1,0:T(8,128)}, f32[2,592,128]{2,1,0:T(8,128)S(1)}, u32[]{:S(2)}, u32[]{:S(2)}) collective-permute-start(f32[2,592,128]{2,1,0:T(8,128)} %get-tuple-element.37), channel_id=1, source_target_pairs={{0,4},{4,8},{8,12},{1,5},{5,9},{9,13},{2,6},{6,10},{10,14},{3,7},{... | collective-permute-start | bytes 1818632 | tf_op jit(solution)/shard_map/ppermute | solution.py:611
  7.7 21.5 %copy-start.14 = (s32[4,4096]{1,0:T(4,128)S(1)}, s32[4,4096]{1,0:T(4,128)}, u32[]{:S(2)}) copy-start(s32[4,4096]{1,0:T(4,128)} %param.17) | copy-start | bytes 196612
  7.7 11.7 %collective-permute-start.1 = (f32[2,592,128]{2,1,0:T(8,128)}, f32[2,592,128]{2,1,0:T(8,128)S(1)}, u32[]{:S(2)}, u32[]{:S(2)}) collective-permute-start(f32[2,592,128]{2,1,0:T(8,128)} %get-tuple-element.38), channel_id=1, source_target_pairs={{4,0},{8,4},{12,8},{5,1},{9,5},{13,9},{6,2},{10,6},{14,10},{7,3},{... | collective-permute-start | bytes 1818632 | tf_op jit(solution)/shard_map/ppermute | solution.py:611
  16.6 13.3 %copy-start.3 = (f32[2,592,128]{2,1,0:T(8,128)}, f32[2,592,128]{2,1,0:T(8,128)S(1)}, u32[]{:S(2)}) copy-start(f32[2,592,128]{2,1,0:T(8,128)S(1)} %collective-permute-done.hs_ref) | copy-start | bytes 1818628
  19.4 10.4 %copy-start.4 = (f32[2,592,128]{2,1,0:T(8,128)}, f32[2,592,128]{2,1,0:T(8,128)S(1)}, u32[]{:S(2)}) copy-start(f32[2,592,128]{2,1,0:T(8,128)S(1)} %collective-permute-done.1.hn_ref) | copy-start | bytes 1818628
  19.4 29.4 %collective-permute-start.4 = (f32[7,592,128]{2,1,0:T(8,128)}, f32[7,592,128]{2,1,0:T(8,128)S(1)}, u32[]{:S(2)}, u32[]{:S(2)}) collective-permute-start(f32[7,592,128]{2,1,0:T(8,128)} %get-tuple-element.46), channel_id=1, source_target_pairs={{0,4},{4,8},{8,12},{1,5},{5,9},{9,13},{2,6},{6,10},{10,14},{3,7},{... | collective-permute-start | bytes 6365192 | tf_op jit(solution)/shard_map/ppermute | solution.py:611
  21.4 27.9 %collective-permute-start.5 = (f32[7,592,128]{2,1,0:T(8,128)}, f32[7,592,128]{2,1,0:T(8,128)}, u32[]{:S(2)}, u32[]{:S(2)}) collective-permute-start(f32[7,592,128]{2,1,0:T(8,128)} %get-tuple-element.47), channel_id=1, source_target_pairs={{4,0},{8,4},{12,8},{5,1},{9,5},{13,9},{6,2},{10,6},{14,10},{7,3},{... | collective-permute-start | bytes 6365192 | tf_op jit(solution)/shard_map/ppermute | solution.py:611
  23.9 18.7 %collective-permute-start.2 = (f32[1152,128]{1,0:T(8,128)}, f32[1152,128]{1,0:T(8,128)}, u32[]{:S(2)}, u32[]{:S(2)}) collective-permute-start(f32[1152,128]{1,0:T(8,128)} %get-tuple-element.41), channel_id=1, source_target_pairs={{0,1},{1,2},{2,3},{4,5},{5,6},{6,7},{8,9},{9,10},{10,11},{12,13},{... | collective-permute-start | bytes 1769480 | tf_op jit(solution)/shard_map/ppermute | solution.py:611
  27.9 17.4 %collective-permute-start.3 = (f32[1152,128]{1,0:T(8,128)}, f32[1152,128]{1,0:T(8,128)}, u32[]{:S(2)}, u32[]{:S(2)}) collective-permute-start(f32[1152,128]{1,0:T(8,128)} %get-tuple-element.42), channel_id=1, source_target_pairs={{1,0},{2,1},{3,2},{5,4},{6,5},{7,6},{9,8},{10,9},{11,10},{13,12},{... | collective-permute-start | bytes 1769480 | tf_op jit(solution)/shard_map/ppermute | solution.py:611
  45.3 31.6 %all-to-all-start = ((f32[4,72,8,128]{3,2,1,0:T(8,128)}), f32[4,72,8,128]{3,2,1,0:T(8,128)S(1)}, u32[]{:S(2)}, u32[]{:S(2)}) async-start(f32[4,72,8,128]{3,2,1,0:T(8,128)} %front.4), calls=%async_computation | async-start | bytes 2359296 | tf_op jit(solution)/shard_map/all_to_all | solution.py:644
  48.9 1.3 copy-start.1
  63.0 32.2 %collective-permute-start.8 = (f32[72,8,128]{2,1,0:T(8,128)}, f32[72,8,128]{2,1,0:T(8,128)S(1)}, u32[]{:S(2)}, u32[]{:S(2)}) collective-permute-start(f32[72,8,128]{2,1,0:T(8,128)} %get-tuple-element.52), channel_id=1, source_target_pairs={{0,3},{1,0},{2,1},{3,2},{4,7},{5,4},{6,5},{7,6},{8,11},{9,8},{10,9... | collective-permute-start | bytes 884744 | tf_op jit(solution)/shard_map/ppermute | solution.py:651
  66.2 42.9 %collective-permute-start.7 = (f32[72,8,128]{2,1,0:T(8,128)}, f32[72,8,128]{2,1,0:T(8,128)S(1)}, u32[]{:S(2)}, u32[]{:S(2)}) collective-permute-start(f32[72,8,128]{2,1,0:T(8,128)} %get-tuple-element.51), channel_id=1, source_target_pairs={{0,2},{1,3},{2,0},{3,1},{4,6},{5,7},{6,4},{7,5},{8,10},{9,11},{10,... | collective-permute-start | bytes 884744 | tf_op jit(solution)/shard_map/ppermute | solution.py:651
  66.2 42.9 %collective-permute-start.6 = (f32[72,8,128]{2,1,0:T(8,128)}, f32[72,8,128]{2,1,0:T(8,128)S(1)}, u32[]{:S(2)}, u32[]{:S(2)}) collective-permute-start(f32[72,8,128]{2,1,0:T(8,128)} %get-tuple-element.50), channel_id=1, source_target_pairs={{0,1},{1,2},{2,3},{3,0},{4,5},{5,6},{6,7},{7,4},{8,9},{9,10},{10,1... | collective-permute-start | bytes 884744 | tf_op jit(solution)/shard_map/ppermute | solution.py:651
  77.0 18.2 %copy-start.2 = (f32[4,72,8,128]{3,2,1,0:T(8,128)}, f32[4,72,8,128]{3,2,1,0:T(8,128)S(1)}, u32[]{:S(2)}) copy-start(f32[4,72,8,128]{3,2,1,0:T(8,128)S(1)} %all-to-all-done.refs_0_) | copy-start | bytes 3538948
  95.2 28.0 %copy-start.8 = (f32[72,8,128]{2,1,0:T(8,128)}, f32[72,8,128]{2,1,0:T(8,128)S(1)}, u32[]{:S(2)}) copy-start(f32[72,8,128]{2,1,0:T(8,128)S(1)} %collective-permute-done.8.refs_4_) | copy-start | bytes 884740
  95.2 28.0 %collective-permute-start.11 = (f32[108,8,128]{2,1,0:T(8,128)}, f32[108,8,128]{2,1,0:T(8,128)S(1)}, u32[]{:S(2)}, u32[]{:S(2)}) collective-permute-start(f32[108,8,128]{2,1,0:T(8,128)} %get-tuple-element.60), channel_id=1, source_target_pairs={{0,3},{1,0},{2,1},{3,2},{4,7},{5,4},{6,5},{7,6},{8,11},{9,8},{10,9... | collective-permute-start | bytes 1327112 | tf_op jit(solution)/shard_map/ppermute | solution.py:651
  109.1 14.0 %copy-start.9 = (f32[72,8,128]{2,1,0:T(8,128)}, f32[72,8,128]{2,1,0:T(8,128)S(1)}, u32[]{:S(2)}) copy-start(f32[72,8,128]{2,1,0:T(8,128)S(1)} %collective-permute-done.7.refs_3_) | copy-start | bytes 884740
  109.1 36.1 %collective-permute-start.10 = (f32[108,8,128]{2,1,0:T(8,128)}, f32[108,8,128]{2,1,0:T(8,128)S(1)}, u32[]{:S(2)}, u32[]{:S(2)}) collective-permute-start(f32[108,8,128]{2,1,0:T(8,128)} %get-tuple-element.58), channel_id=1, source_target_pairs={{0,2},{1,3},{2,0},{3,1},{4,6},{5,7},{6,4},{7,5},{8,10},{9,11},{10,... | collective-permute-start | bytes 1327112 | tf_op jit(solution)/shard_map/ppermute | solution.py:651
  109.2 0.8 copy-start.10
  110.0 35.3 %collective-permute-start.9 = (f32[108,8,128]{2,1,0:T(8,128)}, f32[108,8,128]{2,1,0:T(8,128)S(1)}, u32[]{:S(2)}, u32[]{:S(2)}) collective-permute-start(f32[108,8,128]{2,1,0:T(8,128)} %get-tuple-element.56), channel_id=1, source_target_pairs={{0,1},{1,2},{2,3},{3,0},{4,5},{5,6},{6,7},{7,4},{8,9},{9,10},{10,1... | collective-permute-start | bytes 1327112 | tf_op jit(solution)/shard_map/ppermute | solution.py:651
  110.2 47.2 %copy-start.15 = (s32[4,1296]{1,0:T(4,128)S(1)}, s32[4,1296]{1,0:T(4,128)}, u32[]{:S(2)}) copy-start(s32[4,1296]{1,0:T(4,128)} %param.22) | copy-start | bytes 62212
  110.2 48.4 %copy-start.16 = (f32[2,1296]{1,0:T(2,128)S(1)}, f32[2,1296]{1,0:T(2,128)}, u32[]{:S(2)}) copy-start(f32[2,1296]{1,0:T(2,128)} %param.23) | copy-start | bytes 31108
  123.2 46.3 %copy-start.5 = (f32[108,8,128]{2,1,0:T(8,128)}, f32[108,8,128]{2,1,0:T(8,128)S(1)}, u32[]{:S(2)}) copy-start(f32[108,8,128]{2,1,0:T(8,128)S(1)} %collective-permute-done.11.refs_8_) | copy-start | bytes 1327108
  123.2 37.9 %collective-permute-start.14 = (f32[72,8,128]{2,1,0:T(8,128)}, f32[72,8,128]{2,1,0:T(8,128)S(1)}, u32[]{:S(2)}, u32[]{:S(2)}) collective-permute-start(f32[72,8,128]{2,1,0:T(8,128)} %get-tuple-element.68), channel_id=1, source_target_pairs={{0,3},{1,0},{2,1},{3,2},{4,7},{5,4},{6,5},{7,6},{8,11},{9,8},{10,9... | collective-permute-start | bytes 884744 | tf_op jit(solution)/shard_map/ppermute | solution.py:651
  145.2 24.2 %copy-start.6 = (f32[108,8,128]{2,1,0:T(8,128)}, f32[108,8,128]{2,1,0:T(8,128)S(1)}, u32[]{:S(2)}) copy-start(f32[108,8,128]{2,1,0:T(8,128)S(1)} %collective-permute-done.10.refs_7_) | copy-start | bytes 1327108
  145.2 24.2 %collective-permute-start.13 = (f32[72,8,128]{2,1,0:T(8,128)}, f32[72,8,128]{2,1,0:T(8,128)S(1)}, u32[]{:S(2)}, u32[]{:S(2)}) collective-permute-start(f32[72,8,128]{2,1,0:T(8,128)} %get-tuple-element.66), channel_id=1, source_target_pairs={{0,2},{1,3},{2,0},{3,1},{4,6},{5,7},{6,4},{7,5},{8,10},{9,11},{10,... | collective-permute-start | bytes 884744 | tf_op jit(solution)/shard_map/ppermute | solution.py:651
  145.2 24.2 %copy-start.7 = (f32[108,8,128]{2,1,0:T(8,128)}, f32[108,8,128]{2,1,0:T(8,128)S(1)}, u32[]{:S(2)}) copy-start(f32[108,8,128]{2,1,0:T(8,128)S(1)} %collective-permute-done.9.refs_6_) | copy-start | bytes 1327108
  145.2 24.2 %collective-permute-start.12 = (f32[72,8,128]{2,1,0:T(8,128)}, f32[72,8,128]{2,1,0:T(8,128)S(1)}, u32[]{:S(2)}, u32[]{:S(2)}) collective-permute-start(f32[72,8,128]{2,1,0:T(8,128)} %get-tuple-element.64), channel_id=1, source_target_pairs={{0,1},{1,2},{2,3},{3,0},{4,5},{5,6},{6,7},{7,4},{8,9},{9,10},{10,1... | collective-permute-start | bytes 884744 | tf_op jit(solution)/shard_map/ppermute | solution.py:651
  161.1 8.3 %copy-start.11 = (f32[72,8,128]{2,1,0:T(8,128)}, f32[72,8,128]{2,1,0:T(8,128)S(1)}, u32[]{:S(2)}) copy-start(f32[72,8,128]{2,1,0:T(8,128)S(1)} %collective-permute-done.14.refs_12_) | copy-start | bytes 884740
  169.4 0.7 copy-start.12
  169.4 0.8 copy-start.13

commit v2 on v1

--- a/solution.py
+++ b/solution.py
@@ -646,8 +646,7 @@
         here = [blocks[0]]
         for d in range(1, shares):
             rows = blocks[d]
-            if c > 1:
-                rows, _ = lax.optimization_barrier((rows, arrived[-1][d]))
+            rows, _ = lax.optimization_barrier((rows, arrived[-1][d if c > 1 else 0]))
             here.append(lax.ppermute(rows, "bin", [(i, (i + d) % shares) for i in range(shares)]))
         arrived.append(here)
     parts = sum(arrived, [])

time: 197 us -> 189 us (0.959)
  waiting for transfers between devices: 43.5 us -> 28.5 us
  starting transfers between devices: 52.5 us -> 62.5 us
    ppermute x9, waiting for transfers between devices: 27.3 us -> 13.9 us  [fast_on_device(): lax.ppermute(rows, 'bin', [(i, (i + d) % shares) for i in range(shares)])]
    ppermute x9, starting transfers between devices: 32.6 us -> 39.1 us  [fast_on_device(): lax.ppermute(rows, 'bin', [(i, (i + d) % shares) for i in range(shares)])]
    all_to_all x1, waiting for transfers between devices: 10.2 us -> 7.35 us  [fast_on_device(): lax.all_to_all(blocks, 'bin', split_axis=0, concat_axis=0, tiled=True)]
    all_to_all x1, starting transfers between devices: 3.53 us -> 5.65 us  [fast_on_device(): lax.all_to_all(blocks, 'bin', split_axis=0, concat_axis=0, tiled=True)]
  transfers between devices with their start and end apart: 16 -> 16, of which waited for: 6 -> 6; matrix products, arithmetic and copies ran while one was open for 3% -> 3% of each run, Pallas kernels for 33% -> 34%
where the time goes in v2:
time: 189 us; the launch traced here: 186 us
  Pallas kernels  89.2 us (47%)
  starting transfers between devices  62.5 us (33%)
  waiting for transfers between devices  28.5 us (15%)
  local copies, waits for them, and re-layouts  5.75 us (3%)
    pallas_call x4, Pallas kernels, front(): pl.pallas_call(functools.partial(front_kernel, tiles, shares, nloc, kmin,...  56.1 us
    ppermute x9, starting transfers between devices, fast_on_device(): lax.ppermute(rows, 'bin', [(i, (i + d) % shares) for i in range(shares)])  39.1 us
    pallas_call x1, Pallas kernels, tail(): pl.pallas_call(functools.partial(tail_kernel, nfreq, bins_dev, plan), out...  23.2 us
    ppermute x6, starting transfers between devices, line(): return lax.ppermute(array, axis, pairs)  17.7 us
    ppermute x9, waiting for transfers between devices, fast_on_device(): lax.ppermute(rows, 'bin', [(i, (i + d) % shares) for i in range(shares)])  13.9 us
    pallas_call x2, Pallas kernels, prep(): pl.pallas_call(functools.partial(prep_kernel, points, bins, blocks, group...  9.92 us
    all_to_all x1, waiting for transfers between devices, fast_on_device(): lax.all_to_all(blocks, 'bin', split_axis=0, concat_axis=0, tiled=True)  7.35 us
    ppermute x6, waiting for transfers between devices, line(): return lax.ppermute(array, axis, pairs)  7.18 us
  transfers between devices with their start and end apart: 16, of which 6 were waited for; matrix products, arithmetic and copies ran while one was open for 3% of the time, Pallas kernels for 34%

profile of v2, /device:TPU:1, one launch (start us, length us, event | category | flops | bytes accessed | tf_op | source)
XLA Modules:
  0.0 186.2 jit_solution(12564815031171903315)
XLA Ops:
  0.0 0.0 copy-start
  0.0 3.2 %prep.2 = (f32[2,592,128]{2,1,0:T(8,128)}, f32[2,592,128]{2,1,0:T(8,128)}) custom-call(f32[324,4096]{1,0:T(8,128)} %spec_hbm.2, s32[1,4096]{1,0:T(1,128)} %bitcast.54), custom_call_target="tpu_custom_call" | custom-call | bytes 6000000 | tf_op jit(solution)/shard_map/prep/pallas_call | solution.py:300
  3.2 4.5 %collective-permute-start = (f32[2,592,128]{2,1,0:T(8,128)}, f32[2,592,128]{2,1,0:T(8,128)S(1)}, u32[]{:S(2)}, u32[]{:S(2)}) collective-permute-start(f32[2,592,128]{2,1,0:T(8,128)} %get-tuple-element.40), channel_id=1, source_target_pairs={{0,4},{4,8},{8,12},{1,5},{5,9},{9,13},{2,6},{6,10},{10,14},{3,7},{... | collective-permute-start | bytes 1818632 | tf_op jit(solution)/shard_map/ppermute | solution.py:611
  7.7 0.0 copy-start.14
  7.7 2.1 %collective-permute-start.1 = (f32[2,592,128]{2,1,0:T(8,128)}, f32[2,592,128]{2,1,0:T(8,128)S(1)}, u32[]{:S(2)}, u32[]{:S(2)}) collective-permute-start(f32[2,592,128]{2,1,0:T(8,128)} %get-tuple-element.41), channel_id=1, source_target_pairs={{4,0},{8,4},{12,8},{5,1},{9,5},{13,9},{6,2},{10,6},{14,10},{7,3},{... | collective-permute-start | bytes 1818632 | tf_op jit(solution)/shard_map/ppermute | solution.py:611
  9.8 6.8 %prep.3 = (f32[7,592,128]{2,1,0:T(8,128)}, f32[7,592,128]{2,1,0:T(8,128)}, f32[10368,128]{1,0:T(8,128)}, f32[1152,128]{1,0:T(8,128)}, f32[1152,128]{1,0:T(8,128)}) custom-call(f32[324,4096]{1,0:T(8,128)} %spec_hbm.2, s32[1,4096]{1,0:T(1,128)} %bitcast.55), custom_call_target="tpu_custom_call" | custom-call | bytes 27000000 | tf_op jit(solution)/shard_map/prep/pallas_call | solution.py:300
  16.6 4.0 %collective-permute-start.2 = (f32[1152,128]{1,0:T(8,128)}, f32[1152,128]{1,0:T(8,128)}, u32[]{:S(2)}, u32[]{:S(2)}) collective-permute-start(f32[1152,128]{1,0:T(8,128)} %get-tuple-element.44), channel_id=1, source_target_pairs={{0,1},{1,2},{2,3},{4,5},{5,6},{6,7},{8,9},{9,10},{10,11},{12,13},{... | collective-permute-start | bytes 1769480 | tf_op jit(solution)/shard_map/ppermute | solution.py:611
  20.6 1.3 collective-permute-start.3
  21.9 0.0 collective-permute-done.hs_ref
  21.9 0.0 copy-start.3
  21.9 0.0 collective-permute-done.1.hn_ref
  21.9 0.0 copy-start.4
  21.9 3.9 %collective-permute-start.4 = (f32[7,592,128]{2,1,0:T(8,128)}, f32[7,592,128]{2,1,0:T(8,128)S(1)}, u32[]{:S(2)}, u32[]{:S(2)}) collective-permute-start(f32[7,592,128]{2,1,0:T(8,128)} %get-tuple-element.49), channel_id=1, source_target_pairs={{0,4},{4,8},{8,12},{1,5},{5,9},{9,13},{2,6},{6,10},{10,14},{3,7},{... | collective-permute-start | bytes 6365192 | tf_op jit(solution)/shard_map/ppermute | solution.py:611
  25.8 1.9 %collective-permute-start.5 = (f32[7,592,128]{2,1,0:T(8,128)}, f32[7,592,128]{2,1,0:T(8,128)}, u32[]{:S(2)}, u32[]{:S(2)}) collective-permute-start(f32[7,592,128]{2,1,0:T(8,128)} %get-tuple-element.50), channel_id=1, source_target_pairs={{4,0},{8,4},{12,8},{5,1},{9,5},{13,9},{6,2},{10,6},{14,10},{7,3},{... | collective-permute-start | bytes 6365192 | tf_op jit(solution)/shard_map/ppermute | solution.py:611
  27.8 0.0 copy-done.14
  27.8 0.6 copy.21
  28.4 0.0 copy-done.3
  28.4 0.0 copy-done.4
  28.4 12.7 %front.4 = f32[4,72,8,128]{3,2,1,0:T(8,128)} custom-call(f32[36]{0:T(128)} %constant.21.clone.tab_ref, f32[2,36]{1,0:T(2,128)} %constant.24.clone.dir_ref, s32[1]{0:T(128)} %bitcast.2.pos_ref, s32[4,32,128]{2,1,0:T(8,128)} %bitcast.34, f32[32,128]{1,0:T(8,128)} %bitcast.38, f32[32,128]{1,0:T(8,128)} %bitcast.42, f32[32,128]{1,0:T(8,128)} %bitcast.46, ...), custom_call_target="tpu_custom_call" | custom-call | bytes 44000000 | tf_op jit(solution)/shard_map/front/pallas_call | solution.py:440
  41.1 0.0 collective-permute-done.2
  41.1 0.0 collective-permute-done.3
  41.1 5.6 %all-to-all-start = ((f32[4,72,8,128]{3,2,1,0:T(8,128)}), f32[4,72,8,128]{3,2,1,0:T(8,128)S(1)}, u32[]{:S(2)}, u32[]{:S(2)}) async-start(f32[4,72,8,128]{3,2,1,0:T(8,128)} %front.4), calls=%async_computation | async-start | bytes 2359296 | tf_op jit(solution)/shard_map/all_to_all | solution.py:644
  46.8 2.6 %collective-permute-done.4.hs_ref = f32[7,592,128]{2,1,0:T(8,128)S(1)} collective-permute-done((f32[7,592,128]{2,1,0:T(8,128)}, f32[7,592,128]{2,1,0:T(8,128)S(1)}, u32[]{:S(2)}, u32[]{:S(2)}) %collective-permute-start.4) | collective-permute-done | bytes 2121760 | tf_op jit(solution)/shard_map/ppermute | solution.py:611
  49.4 4.6 %collective-permute-done.5.hn_ref = f32[7,592,128]{2,1,0:T(8,128)} collective-permute-done((f32[7,592,128]{2,1,0:T(8,128)}, f32[7,592,128]{2,1,0:T(8,128)}, u32[]{:S(2)}, u32[]{:S(2)}) %collective-permute-start.5) | collective-permute-done | bytes 2121760 | tf_op jit(solution)/shard_map/ppermute | solution.py:611
  54.0 0.0 copy-done.1
  54.0 12.7 %front.5 = (f32[72,8,128]{2,1,0:T(8,128)}, f32[72,8,128]{2,1,0:T(8,128)}, f32[72,8,128]{2,1,0:T(8,128)}, f32[72,8,128]{2,1,0:T(8,128)}) custom-call(f32[36]{0:T(128)} %constant.21.clone.tab_ref, f32[2,36]{1,0:T(2,128)} %constant.24.clone.dir_ref, s32[1]{0:T(128)} %bitcast.2.pos_ref, s32[4,32,128]{2,1,0:T(8,128)} %bitcast.35, f32[32,128]{1,0:T(8,128)} %bitcast.39, ...), custom_call_target="tpu_custom_call" | custom-call | bytes 44000000 | tf_op jit(solution)/shard_map/front/pallas_call | solution.py:440
  66.7 7.3 %all-to-all-done.refs_0_ = f32[4,72,8,128]{3,2,1,0:T(8,128)S(1)} async-done(((f32[4,72,8,128]{3,2,1,0:T(8,128)}), f32[4,72,8,128]{3,2,1,0:T(8,128)S(1)}, u32[]{:S(2)}, u32[]{:S(2)}) %all-to-all-start) | async-done | bytes 1179680 | tf_op jit(solution)/shard_map/all_to_all | solution.py:644
  74.0 1.2 collective-permute-start.8
  75.2 0.0 collective-permute-start.7
  75.2 0.3 collective-permute-start.6
  75.5 17.8 %front.6 = (f32[108,8,128]{2,1,0:T(8,128)}, f32[108,8,128]{2,1,0:T(8,128)}, f32[108,8,128]{2,1,0:T(8,128)}, f32[108,8,128]{2,1,0:T(8,128)}) custom-call(f32[36]{0:T(128)} %constant.21.clone.tab_ref, f32[2,36]{1,0:T(2,128)} %constant.24.clone.dir_ref, s32[1]{0:T(128)} %bitcast.2.pos_ref, s32[4,32,128]{2,1,0:T(8,128)} %bitcast.36, f32[32,128]{1,0:T(8,128)} %bitcast.40, ...), custom_call_target="tpu_custom_call" | custom-call | bytes 66000000 | tf_op jit(solution)/shard_map/front/pallas_call | solution.py:440
  93.3 0.0 copy-done.2
  93.3 0.0 collective-permute-done.8.refs_4_
  93.3 0.0 copy-start.8
  93.3 3.0 %collective-permute-start.11 = (f32[108,8,128]{2,1,0:T(8,128)}, f32[108,8,128]{2,1,0:T(8,128)S(1)}, u32[]{:S(2)}, u32[]{:S(2)}) collective-permute-start(f32[108,8,128]{2,1,0:T(8,128)} %get-tuple-element.66), channel_id=1, source_target_pairs={{0,3},{1,0},{2,1},{3,2},{4,7},{5,4},{6,5},{7,6},{8,11},{9,8},{10,9... | collective-permute-start | bytes 1327112 | tf_op jit(solution)/shard_map/ppermute | solution.py:650
  96.4 4.0 %collective-permute-done.7.refs_3_ = f32[72,8,128]{2,1,0:T(8,128)S(1)} collective-permute-done((f32[72,8,128]{2,1,0:T(8,128)}, f32[72,8,128]{2,1,0:T(8,128)S(1)}, u32[]{:S(2)}, u32[]{:S(2)}) %collective-permute-start.7) | collective-permute-done | bytes 294944 | tf_op jit(solution)/shard_map/ppermute | solution.py:650
  100.4 0.0 collective-permute-start.10
  100.4 0.0 collective-permute-done.6.refs_2_
  100.4 0.0 copy-start.10
  100.5 20.1 %collective-permute-start.9 = (f32[108,8,128]{2,1,0:T(8,128)}, f32[108,8,128]{2,1,0:T(8,128)S(1)}, u32[]{:S(2)}, u32[]{:S(2)}) collective-permute-start(f32[108,8,128]{2,1,0:T(8,128)} %get-tuple-element.62), channel_id=1, source_target_pairs={{0,1},{1,2},{2,3},{3,0},{4,5},{5,6},{6,7},{7,4},{8,9},{9,10},{10,1... | collective-permute-start | bytes 1327112 | tf_op jit(solution)/shard_map/ppermute | solution.py:650
  120.5 12.9 %front.7 = (f32[72,8,128]{2,1,0:T(8,128)}, f32[72,8,128]{2,1,0:T(8,128)}, f32[72,8,128]{2,1,0:T(8,128)}, f32[72,8,128]{2,1,0:T(8,128)}) custom-call(f32[36]{0:T(128)} %constant.21.clone.tab_ref, f32[2,36]{1,0:T(2,128)} %constant.24.clone.dir_ref, s32[1]{0:T(128)} %bitcast.2.pos_ref, s32[4,32,128]{2,1,0:T(8,128)} %bitcast.37, f32[32,128]{1,0:T(8,128)} %bitcast.41, ...), custom_call_target="tpu_custom_call" | custom-call | bytes 44000000 | tf_op jit(solution)/shard_map/front/pallas_call | solution.py:440
  133.5 0.0 copy-done.8
  133.5 0.0 copy-done.9
  133.5 0.0 copy-done.10
  133.5 0.0 collective-permute-done.11.refs_8_
  133.5 0.1 collective-permute-start.14
  133.6 4.2 %collective-permute-done.10.refs_7_ = f32[108,8,128]{2,1,0:T(8,128)S(1)} collective-permute-done((f32[108,8,128]{2,1,0:T(8,128)}, f32[108,8,128]{2,1,0:T(8,128)S(1)}, u32[]{:S(2)}, u32[]{:S(2)}) %collective-permute-start.10) | collective-permute-done | bytes 442400 | tf_op jit(solution)/shard_map/ppermute | solution.py:650
  137.7 0.0 collective-permute-start.13
  137.7 0.0 collective-permute-done.9.refs_6_
  137.7 0.0 copy-start.7
  137.7 14.4 %collective-permute-start.12 = (f32[72,8,128]{2,1,0:T(8,128)}, f32[72,8,128]{2,1,0:T(8,128)S(1)}, u32[]{:S(2)}, u32[]{:S(2)}) collective-permute-start(f32[72,8,128]{2,1,0:T(8,128)} %get-tuple-element.70), channel_id=1, source_target_pairs={{0,1},{1,2},{2,3},{3,0},{4,5},{5,6},{6,7},{7,4},{8,9},{9,10},{10,1... | collective-permute-start | bytes 884744 | tf_op jit(solution)/shard_map/ppermute | solution.py:650
  152.2 0.6 copy.22
  152.8 0.3 copy.15
  153.1 1.0 reshape.42.spot_ref
  154.0 0.0 copy-done.16
  154.0 0.3 copy.16
  154.3 0.9 reshape.43.wts_ref
  155.2 1.3 dynamic-slice_bitcast_fusion.1.mask_ref
  156.5 0.0 collective-permute-done.14.refs_12_
  156.5 5.7 %collective-permute-done.13.refs_11_ = f32[72,8,128]{2,1,0:T(8,128)S(1)} collective-permute-done((f32[72,8,128]{2,1,0:T(8,128)}, f32[72,8,128]{2,1,0:T(8,128)S(1)}, u32[]{:S(2)}, u32[]{:S(2)}) %collective-permute-start.13) | collective-permute-done | bytes 294944 | tf_op jit(solution)/shard_map/ppermute | solution.py:650
  162.2 0.0 collective-permute-done.12.refs_10_
  162.3 0.7 copy-done.12
  162.9 0.1 copy-done.13
  163.0 23.2 %tail.1 = f32[1296,1024]{1,0:T(8,128)} custom-call(s32[5184]{0:T(1024)} %reshape.42.spot_ref, f32[2592]{0:T(1024)} %reshape.43.wts_ref, f32[3,36]{1,0:T(4,128)} %constant.22.clone.ftab_ref, f32[1296]{0:T(1024)} %constant.23.clone.frs_ref, f32[2,36]{1,0:T(2,128)} %constant.24.clone.dir_ref, s32[1]{0:T(128)} %bitcast.2.pos_ref, f32[2,8,128]{2,1,0:T(8,128)} %bitcast.56, ...), custom_call_target="tpu_custom_call" | custom-call | bytes 70000000 | tf_op jit(solution)/shard_map/tail/pallas_call | solution.py:555
  (18 shorter events, 0.0 us)
Async XLA Ops:
  0.0 152.2 %copy-start = (f32[2,4096]{1,0:T(2,128)S(1)}, f32[2,4096]{1,0:T(2,128)}, u32[]{:S(2)}) copy-start(f32[2,4096]{1,0:T(2,128)} %param.15) | copy-start | bytes 98308
  3.2 18.7 %collective-permute-start = (f32[2,592,128]{2,1,0:T(8,128)}, f32[2,592,128]{2,1,0:T(8,128)S(1)}, u32[]{:S(2)}, u32[]{:S(2)}) collective-permute-start(f32[2,592,128]{2,1,0:T(8,128)} %get-tuple-element.40), channel_id=1, source_target_pairs={{0,4},{4,8},{8,12},{1,5},{5,9},{9,13},{2,6},{6,10},{10,14},{3,7},{... | collective-permute-start | bytes 1818632 | tf_op jit(solution)/shard_map/ppermute | solution.py:611
  7.7 20.1 %copy-start.14 = (s32[4,4096]{1,0:T(4,128)S(1)}, s32[4,4096]{1,0:T(4,128)}, u32[]{:S(2)}) copy-start(s32[4,4096]{1,0:T(4,128)} %param.17) | copy-start | bytes 196612
  7.7 14.2 %collective-permute-start.1 = (f32[2,592,128]{2,1,0:T(8,128)}, f32[2,592,128]{2,1,0:T(8,128)S(1)}, u32[]{:S(2)}, u32[]{:S(2)}) collective-permute-start(f32[2,592,128]{2,1,0:T(8,128)} %get-tuple-element.41), channel_id=1, source_target_pairs={{4,0},{8,4},{12,8},{5,1},{9,5},{13,9},{6,2},{10,6},{14,10},{7,3},{... | collective-permute-start | bytes 1818632 | tf_op jit(solution)/shard_map/ppermute | solution.py:611
  16.6 24.6 %collective-permute-start.2 = (f32[1152,128]{1,0:T(8,128)}, f32[1152,128]{1,0:T(8,128)}, u32[]{:S(2)}, u32[]{:S(2)}) collective-permute-start(f32[1152,128]{1,0:T(8,128)} %get-tuple-element.44), channel_id=1, source_target_pairs={{0,1},{1,2},{2,3},{4,5},{5,6},{6,7},{8,9},{9,10},{10,11},{12,13},{... | collective-permute-start | bytes 1769480 | tf_op jit(solution)/shard_map/ppermute | solution.py:611
  20.6 20.5 %collective-permute-start.3 = (f32[1152,128]{1,0:T(8,128)}, f32[1152,128]{1,0:T(8,128)}, u32[]{:S(2)}, u32[]{:S(2)}) collective-permute-start(f32[1152,128]{1,0:T(8,128)} %get-tuple-element.45), channel_id=1, source_target_pairs={{1,0},{2,1},{3,2},{5,4},{6,5},{7,6},{9,8},{10,9},{11,10},{13,12},{... | collective-permute-start | bytes 1769480 | tf_op jit(solution)/shard_map/ppermute | solution.py:611
  21.9 6.5 %copy-start.3 = (f32[2,592,128]{2,1,0:T(8,128)}, f32[2,592,128]{2,1,0:T(8,128)S(1)}, u32[]{:S(2)}) copy-start(f32[2,592,128]{2,1,0:T(8,128)S(1)} %collective-permute-done.hs_ref) | copy-start | bytes 1818628
  21.9 6.5 %copy-start.4 = (f32[2,592,128]{2,1,0:T(8,128)}, f32[2,592,128]{2,1,0:T(8,128)S(1)}, u32[]{:S(2)}) copy-start(f32[2,592,128]{2,1,0:T(8,128)S(1)} %collective-permute-done.1.hn_ref) | copy-start | bytes 1818628
  21.9 27.5 %collective-permute-start.4 = (f32[7,592,128]{2,1,0:T(8,128)}, f32[7,592,128]{2,1,0:T(8,128)S(1)}, u32[]{:S(2)}, u32[]{:S(2)}) collective-permute-start(f32[7,592,128]{2,1,0:T(8,128)} %get-tuple-element.49), channel_id=1, source_target_pairs={{0,4},{4,8},{8,12},{1,5},{5,9},{9,13},{2,6},{6,10},{10,14},{3,7},{... | collective-permute-start | bytes 6365192 | tf_op jit(solution)/shard_map/ppermute | solution.py:611
  25.8 28.1 %collective-permute-start.5 = (f32[7,592,128]{2,1,0:T(8,128)}, f32[7,592,128]{2,1,0:T(8,128)}, u32[]{:S(2)}, u32[]{:S(2)}) collective-permute-start(f32[7,592,128]{2,1,0:T(8,128)} %get-tuple-element.50), channel_id=1, source_target_pairs={{4,0},{8,4},{12,8},{5,1},{9,5},{13,9},{6,2},{10,6},{14,10},{7,3},{... | collective-permute-start | bytes 6365192 | tf_op jit(solution)/shard_map/ppermute | solution.py:611
  41.1 32.9 %all-to-all-start = ((f32[4,72,8,128]{3,2,1,0:T(8,128)}), f32[4,72,8,128]{3,2,1,0:T(8,128)S(1)}, u32[]{:S(2)}, u32[]{:S(2)}) async-start(f32[4,72,8,128]{3,2,1,0:T(8,128)} %front.4), calls=%async_computation | async-start | bytes 2359296 | tf_op jit(solution)/shard_map/all_to_all | solution.py:644
  49.4 4.6 %copy-start.1 = (f32[7,592,128]{2,1,0:T(8,128)}, f32[7,592,128]{2,1,0:T(8,128)S(1)}, u32[]{:S(2)}) copy-start(f32[7,592,128]{2,1,0:T(8,128)S(1)} %collective-permute-done.4.hs_ref) | copy-start | bytes 6365188
  74.0 19.3 %copy-start.2 = (f32[4,72,8,128]{3,2,1,0:T(8,128)}, f32[4,72,8,128]{3,2,1,0:T(8,128)S(1)}, u32[]{:S(2)}) copy-start(f32[4,72,8,128]{3,2,1,0:T(8,128)S(1)} %all-to-all-done.refs_0_) | copy-start | bytes 3538948
  74.0 19.3 %collective-permute-start.8 = (f32[72,8,128]{2,1,0:T(8,128)}, f32[72,8,128]{2,1,0:T(8,128)S(1)}, u32[]{:S(2)}, u32[]{:S(2)}) collective-permute-start(f32[72,8,128]{2,1,0:T(8,128)} %get-tuple-element.58), channel_id=1, source_target_pairs={{0,3},{1,0},{2,1},{3,2},{4,7},{5,4},{6,5},{7,6},{8,11},{9,8},{10,9... | collective-permute-start | bytes 884744 | tf_op jit(solution)/shard_map/ppermute | solution.py:650
  75.2 25.2 %collective-permute-start.7 = (f32[72,8,128]{2,1,0:T(8,128)}, f32[72,8,128]{2,1,0:T(8,128)S(1)}, u32[]{:S(2)}, u32[]{:S(2)}) collective-permute-start(f32[72,8,128]{2,1,0:T(8,128)} %get-tuple-element.56), channel_id=1, source_target_pairs={{0,2},{1,3},{2,0},{3,1},{4,6},{5,7},{6,4},{7,5},{8,10},{9,11},{10,... | collective-permute-start | bytes 884744 | tf_op jit(solution)/shard_map/ppermute | solution.py:650
  75.2 25.2 %collective-permute-start.6 = (f32[72,8,128]{2,1,0:T(8,128)}, f32[72,8,128]{2,1,0:T(8,128)S(1)}, u32[]{:S(2)}, u32[]{:S(2)}) collective-permute-start(f32[72,8,128]{2,1,0:T(8,128)} %get-tuple-element.54), channel_id=1, source_target_pairs={{0,1},{1,2},{2,3},{3,0},{4,5},{5,6},{6,7},{7,4},{8,9},{9,10},{10,1... | collective-permute-start | bytes 884744 | tf_op jit(solution)/shard_map/ppermute | solution.py:650
  93.3 40.1 %copy-start.8 = (f32[72,8,128]{2,1,0:T(8,128)}, f32[72,8,128]{2,1,0:T(8,128)S(1)}, u32[]{:S(2)}) copy-start(f32[72,8,128]{2,1,0:T(8,128)S(1)} %collective-permute-done.8.refs_4_) | copy-start | bytes 884740
  93.3 40.1 %collective-permute-start.11 = (f32[108,8,128]{2,1,0:T(8,128)}, f32[108,8,128]{2,1,0:T(8,128)S(1)}, u32[]{:S(2)}, u32[]{:S(2)}) collective-permute-start(f32[108,8,128]{2,1,0:T(8,128)} %get-tuple-element.66), channel_id=1, source_target_pairs={{0,3},{1,0},{2,1},{3,2},{4,7},{5,4},{6,5},{7,6},{8,11},{9,8},{10,9... | collective-permute-start | bytes 1327112 | tf_op jit(solution)/shard_map/ppermute | solution.py:650
  100.4 33.0 %copy-start.9 = (f32[72,8,128]{2,1,0:T(8,128)}, f32[72,8,128]{2,1,0:T(8,128)S(1)}, u32[]{:S(2)}) copy-start(f32[72,8,128]{2,1,0:T(8,128)S(1)} %collective-permute-done.7.refs_3_) | copy-start | bytes 884740
  100.4 37.3 %collective-permute-start.10 = (f32[108,8,128]{2,1,0:T(8,128)}, f32[108,8,128]{2,1,0:T(8,128)S(1)}, u32[]{:S(2)}, u32[]{:S(2)}) collective-permute-start(f32[108,8,128]{2,1,0:T(8,128)} %get-tuple-element.64), channel_id=1, source_target_pairs={{0,2},{1,3},{2,0},{3,1},{4,6},{5,7},{6,4},{7,5},{8,10},{9,11},{10,... | collective-permute-start | bytes 1327112 | tf_op jit(solution)/shard_map/ppermute | solution.py:650
  100.4 33.0 %copy-start.10 = (f32[72,8,128]{2,1,0:T(8,128)}, f32[72,8,128]{2,1,0:T(8,128)S(1)}, u32[]{:S(2)}) copy-start(f32[72,8,128]{2,1,0:T(8,128)S(1)} %collective-permute-done.6.refs_2_) | copy-start | bytes 884740
  100.5 37.3 %collective-permute-start.9 = (f32[108,8,128]{2,1,0:T(8,128)}, f32[108,8,128]{2,1,0:T(8,128)S(1)}, u32[]{:S(2)}, u32[]{:S(2)}) collective-permute-start(f32[108,8,128]{2,1,0:T(8,128)} %get-tuple-element.62), channel_id=1, source_target_pairs={{0,1},{1,2},{2,3},{3,0},{4,5},{5,6},{6,7},{7,4},{8,9},{9,10},{10,1... | collective-permute-start | bytes 1327112 | tf_op jit(solution)/shard_map/ppermute | solution.py:650
  120.5 32.2 %copy-start.15 = (s32[4,1296]{1,0:T(4,128)S(1)}, s32[4,1296]{1,0:T(4,128)}, u32[]{:S(2)}) copy-start(s32[4,1296]{1,0:T(4,128)} %param.22) | copy-start | bytes 62212
  120.5 33.5 %copy-start.16 = (f32[2,1296]{1,0:T(2,128)S(1)}, f32[2,1296]{1,0:T(2,128)}, u32[]{:S(2)}) copy-start(f32[2,1296]{1,0:T(2,128)} %param.23) | copy-start | bytes 31108
  133.5 28.7 %copy-start.5 = (f32[108,8,128]{2,1,0:T(8,128)}, f32[108,8,128]{2,1,0:T(8,128)S(1)}, u32[]{:S(2)}) copy-start(f32[108,8,128]{2,1,0:T(8,128)S(1)} %collective-permute-done.11.refs_8_) | copy-start | bytes 1327108
  133.5 23.0 %collective-permute-start.14 = (f32[72,8,128]{2,1,0:T(8,128)}, f32[72,8,128]{2,1,0:T(8,128)S(1)}, u32[]{:S(2)}, u32[]{:S(2)}) collective-permute-start(f32[72,8,128]{2,1,0:T(8,128)} %get-tuple-element.74), channel_id=1, source_target_pairs={{0,3},{1,0},{2,1},{3,2},{4,7},{5,4},{6,5},{7,6},{8,11},{9,8},{10,9... | collective-permute-start | bytes 884744 | tf_op jit(solution)/shard_map/ppermute | solution.py:650
  137.7 24.5 %copy-start.6 = (f32[108,8,128]{2,1,0:T(8,128)}, f32[108,8,128]{2,1,0:T(8,128)S(1)}, u32[]{:S(2)}) copy-start(f32[108,8,128]{2,1,0:T(8,128)S(1)} %collective-permute-done.10.refs_7_) | copy-start | bytes 1327108
  137.7 24.5 %collective-permute-start.13 = (f32[72,8,128]{2,1,0:T(8,128)}, f32[72,8,128]{2,1,0:T(8,128)S(1)}, u32[]{:S(2)}, u32[]{:S(2)}) collective-permute-start(f32[72,8,128]{2,1,0:T(8,128)} %get-tuple-element.72), channel_id=1, source_target_pairs={{0,2},{1,3},{2,0},{3,1},{4,6},{5,7},{6,4},{7,5},{8,10},{9,11},{10,... | collective-permute-start | bytes 884744 | tf_op jit(solution)/shard_map/ppermute | solution.py:650
  137.7 24.5 %copy-start.7 = (f32[108,8,128]{2,1,0:T(8,128)}, f32[108,8,128]{2,1,0:T(8,128)S(1)}, u32[]{:S(2)}) copy-start(f32[108,8,128]{2,1,0:T(8,128)S(1)} %collective-permute-done.9.refs_6_) | copy-start | bytes 1327108
  137.7 24.5 %collective-permute-start.12 = (f32[72,8,128]{2,1,0:T(8,128)}, f32[72,8,128]{2,1,0:T(8,128)S(1)}, u32[]{:S(2)}, u32[]{:S(2)}) collective-permute-start(f32[72,8,128]{2,1,0:T(8,128)} %get-tuple-element.70), channel_id=1, source_target_pairs={{0,1},{1,2},{2,3},{3,0},{4,5},{5,6},{6,7},{7,4},{8,9},{9,10},{10,1... | collective-permute-start | bytes 884744 | tf_op jit(solution)/shard_map/ppermute | solution.py:650
  156.5 5.8 %copy-start.11 = (f32[72,8,128]{2,1,0:T(8,128)}, f32[72,8,128]{2,1,0:T(8,128)S(1)}, u32[]{:S(2)}) copy-start(f32[72,8,128]{2,1,0:T(8,128)S(1)} %collective-permute-done.14.refs_12_) | copy-start | bytes 884740
  162.2 0.7 copy-start.12
  162.2 0.8 copy-start.13

commit v3 on v2

--- a/solution.py
+++ b/solution.py
@@ -176,12 +176,7 @@
 
 def chunk_plan(nloc):
     mid = nloc // 2
-    plan = [(mid - d, 2 * d, 2) for d in range(1, mid + 1)]
-    if mid > 3:
-        plan[2] = (mid - 3, 3, 3)
-    else:
-        plan.insert(0, (mid, 1, 1))
-    return plan
+    return [(mid, 1, 1)] + [(mid - d, 2 * d, 2) for d in range(1, mid + 1)]
 
 
 def freqs_of(chunk):

time: 189 us -> 193 us (1.021); the launches traced: 186 us -> 192 us
  waiting for transfers between devices: 28.5 us -> 59.6 us
  starting transfers between devices: 62.5 us -> 34.8 us
  Pallas kernels: 89.2 us -> 91.7 us
    ppermute x9 -> x12, waiting for transfers between devices: 13.9 us -> 46.3 us  [fast_on_device(): lax.ppermute(rows, 'bin', [(i, (i + d) % shares) for i in range(shares)])]
    ppermute x9 -> x12, starting transfers between devices: 39.1 us -> 14.6 us  [fast_on_device(): lax.ppermute(rows, 'bin', [(i, (i + d) % shares) for i in range(shares)])]
    all_to_all x1, waiting for transfers between devices: 7.35 us -> 0.01 us  [fast_on_device(): lax.all_to_all(blocks, 'bin', split_axis=0, concat_axis=0, tiled=True)]
    ppermute x6, waiting for transfers between devices: 7.18 us -> 13.3 us  [line(): return lax.ppermute(array, axis, pairs)]
    pallas_call x4 -> x5, Pallas kernels: 56.1 us -> 58.7 us  [front(): pl.pallas_call(functools.partial(front_kernel, tiles, shares, nloc, kmin,...]
    all_to_all x1, starting transfers between devices: 5.65 us -> 3.55 us  [fast_on_device(): lax.all_to_all(blocks, 'bin', split_axis=0, concat_axis=0, tiled=True)]
  transfers between devices with their start and end apart: 16 -> 19, of which waited for: 6 -> 7; matrix products, arithmetic and copies ran while one was open for 3% -> 3% of each run, Pallas kernels for 34% -> 34%
where the time goes in v3:
time: 193 us; the launch traced here: 192 us
  Pallas kernels  91.7 us (48%)
  waiting for transfers between devices  59.6 us (31%)
  starting transfers between devices  34.8 us (18%)
  local copies, waits for them, and re-layouts  5.92 us (3%)
    pallas_call x5, Pallas kernels, front(): pl.pallas_call(functools.partial(front_kernel, tiles, shares, nloc, kmin,...  58.7 us
    ppermute x12, waiting for transfers between devices, fast_on_device(): lax.ppermute(rows, 'bin', [(i, (i + d) % shares) for i in range(shares)])  46.3 us
    pallas_call x1, Pallas kernels, tail(): pl.pallas_call(functools.partial(tail_kernel, nfreq, bins_dev, plan), out...  23.2 us
    ppermute x6, starting transfers between devices, line(): return lax.ppermute(array, axis, pairs)  16.7 us
    ppermute x12, starting transfers between devices, fast_on_device(): lax.ppermute(rows, 'bin', [(i, (i + d) % shares) for i in range(shares)])  14.6 us
    ppermute x6, waiting for transfers between devices, line(): return lax.ppermute(array, axis, pairs)  13.3 us
    pallas_call x2, Pallas kernels, prep(): pl.pallas_call(functools.partial(prep_kernel, points, bins, blocks, group...  9.86 us
  transfers between devices with their start and end apart: 19, of which 7 were waited for; matrix products, arithmetic and copies ran while one was open for 3% of the time, Pallas kernels for 34%

profile of v3, /device:TPU:1, one launch (start us, length us, event | category | flops | bytes accessed | tf_op | source)
XLA Modules:
  0.0 192.5 jit_solution(5648373303685499053)
XLA Ops:
  0.0 0.0 copy-start
  0.0 2.9 %prep.2 = (f32[1,592,128]{2,1,0:T(8,128)}, f32[1,592,128]{2,1,0:T(8,128)}) custom-call(f32[324,4096]{1,0:T(8,128)} %spec_hbm.2, s32[1,4096]{1,0:T(1,128)} %bitcast.63), custom_call_target="tpu_custom_call" | custom-call | bytes 3000000 | tf_op jit(solution)/shard_map/prep/pallas_call | solution.py:295
  2.9 4.5 %collective-permute-start = (f32[1,592,128]{2,1,0:T(8,128)}, f32[1,592,128]{2,1,0:T(8,128)S(1)}, u32[]{:S(2)}, u32[]{:S(2)}) collective-permute-start(f32[1,592,128]{2,1,0:T(8,128)} %get-tuple-element.48), channel_id=1, source_target_pairs={{0,4},{4,8},{8,12},{1,5},{5,9},{9,13},{2,6},{6,10},{10,14},{3,7},{... | collective-permute-start | bytes 909320 | tf_op jit(solution)/shard_map/ppermute | solution.py:606
  7.4 0.0 copy-start.18
  7.5 2.1 %collective-permute-start.1 = (f32[1,592,128]{2,1,0:T(8,128)}, f32[1,592,128]{2,1,0:T(8,128)S(1)}, u32[]{:S(2)}, u32[]{:S(2)}) collective-permute-start(f32[1,592,128]{2,1,0:T(8,128)} %get-tuple-element.49), channel_id=1, source_target_pairs={{4,0},{8,4},{12,8},{5,1},{9,5},{13,9},{6,2},{10,6},{14,10},{7,3},{... | collective-permute-start | bytes 909320 | tf_op jit(solution)/shard_map/ppermute | solution.py:606
  9.5 7.0 %prep.3 = (f32[8,592,128]{2,1,0:T(8,128)}, f32[8,592,128]{2,1,0:T(8,128)}, f32[10368,128]{1,0:T(8,128)}, f32[1152,128]{1,0:T(8,128)}, f32[1152,128]{1,0:T(8,128)}) custom-call(f32[324,4096]{1,0:T(8,128)} %spec_hbm.2, s32[1,4096]{1,0:T(1,128)} %bitcast.64), custom_call_target="tpu_custom_call" | custom-call | bytes 27000000 | tf_op jit(solution)/shard_map/prep/pallas_call | solution.py:295
  16.5 0.0 collective-permute-done.hs_ref
  16.5 0.0 collective-permute-done.1.hn_ref
  16.5 3.6 %collective-permute-start.4 = (f32[8,592,128]{2,1,0:T(8,128)}, f32[8,592,128]{2,1,0:T(8,128)S(1)}, u32[]{:S(2)}, u32[]{:S(2)}) collective-permute-start(f32[8,592,128]{2,1,0:T(8,128)} %get-tuple-element.57), channel_id=1, source_target_pairs={{0,4},{4,8},{8,12},{1,5},{5,9},{9,13},{2,6},{6,10},{10,14},{3,7},{... | collective-permute-start | bytes 7274504 | tf_op jit(solution)/shard_map/ppermute | solution.py:606
  20.2 1.9 collective-permute-start.5
  22.1 3.2 %collective-permute-start.2 = (f32[1152,128]{1,0:T(8,128)}, f32[1152,128]{1,0:T(8,128)S(1)}, u32[]{:S(2)}, u32[]{:S(2)}) collective-permute-start(f32[1152,128]{1,0:T(8,128)} %get-tuple-element.52), channel_id=1, source_target_pairs={{0,1},{1,2},{2,3},{4,5},{5,6},{6,7},{8,9},{9,10},{10,11},{12,13},{... | collective-permute-start | bytes 1769480 | tf_op jit(solution)/shard_map/ppermute | solution.py:606
  25.4 1.3 collective-permute-start.3
  26.7 0.6 copy.21
  27.3 0.0 copy-done.4
  27.3 7.4 %front.5 = f32[4,36,8,128]{3,2,1,0:T(8,128)} custom-call(f32[36]{0:T(128)} %constant.21.clone.tab_ref, f32[2,36]{1,0:T(2,128)} %constant.24.clone.dir_ref, s32[1]{0:T(128)} %bitcast.2.pos_ref, s32[4,32,128]{2,1,0:T(8,128)} %bitcast.37, f32[32,128]{1,0:T(8,128)} %bitcast.43, f32[32,128]{1,0:T(8,128)} %bitcast.48, f32[32,128]{1,0:T(8,128)} %bitcast.53, ...), custom_call_target="tpu_custom_call" | custom-call | bytes 22000000 | tf_op jit(solution)/shard_map/front/pallas_call | solution.py:435
  34.7 2.8 %collective-permute-done.2 = f32[1152,128]{1,0:T(8,128)S(1)} collective-permute-done((f32[1152,128]{1,0:T(8,128)}, f32[1152,128]{1,0:T(8,128)S(1)}, u32[]{:S(2)}, u32[]{:S(2)}) %collective-permute-start.2) | collective-permute-done | bytes 589856 | tf_op jit(solution)/shard_map/ppermute | solution.py:606
  37.5 4.1 %collective-permute-done.3 = f32[1152,128]{1,0:T(8,128)} collective-permute-done((f32[1152,128]{1,0:T(8,128)}, f32[1152,128]{1,0:T(8,128)}, u32[]{:S(2)}, u32[]{:S(2)}) %collective-permute-start.3) | collective-permute-done | bytes 589856 | tf_op jit(solution)/shard_map/ppermute | solution.py:606
  41.7 0.0 copy-done.3
  41.7 3.5 %all-to-all-start = ((f32[4,36,8,128]{3,2,1,0:T(8,128)}), f32[4,36,8,128]{3,2,1,0:T(8,128)S(1)}, u32[]{:S(2)}, u32[]{:S(2)}) async-start(f32[4,36,8,128]{3,2,1,0:T(8,128)} %front.5), calls=%async_computation | async-start | bytes 1179648 | tf_op jit(solution)/shard_map/all_to_all | solution.py:639
  45.2 1.7 collective-permute-done.4.hs_ref
  47.0 4.6 %collective-permute-done.5.hn_ref = f32[8,592,128]{2,1,0:T(8,128)} collective-permute-done((f32[8,592,128]{2,1,0:T(8,128)}, f32[8,592,128]{2,1,0:T(8,128)}, u32[]{:S(2)}, u32[]{:S(2)}) %collective-permute-start.5) | collective-permute-done | bytes 2424864 | tf_op jit(solution)/shard_map/ppermute | solution.py:606
  51.6 12.8 %front.6 = (f32[72,8,128]{2,1,0:T(8,128)}, f32[72,8,128]{2,1,0:T(8,128)}, f32[72,8,128]{2,1,0:T(8,128)}, f32[72,8,128]{2,1,0:T(8,128)}) custom-call(f32[36]{0:T(128)} %constant.21.clone.tab_ref, f32[2,36]{1,0:T(2,128)} %constant.24.clone.dir_ref, s32[1]{0:T(128)} %bitcast.2.pos_ref, s32[4,32,128]{2,1,0:T(8,128)} %bitcast.38, f32[32,128]{1,0:T(8,128)} %bitcast.44, ...), custom_call_target="tpu_custom_call" | custom-call | bytes 44000000 | tf_op jit(solution)/shard_map/front/pallas_call | solution.py:435
  64.3 0.0 all-to-all-done.refs_0_
  64.4 3.4 %collective-permute-start.8 = (f32[72,8,128]{2,1,0:T(8,128)}, f32[72,8,128]{2,1,0:T(8,128)S(1)}, u32[]{:S(2)}, u32[]{:S(2)}) collective-permute-start(f32[72,8,128]{2,1,0:T(8,128)} %get-tuple-element.66), channel_id=1, source_target_pairs={{0,3},{1,0},{2,1},{3,2},{4,7},{5,4},{6,5},{7,6},{8,11},{9,8},{10,9... | collective-permute-start | bytes 884744 | tf_op jit(solution)/shard_map/ppermute | solution.py:645
  67.7 0.0 collective-permute-start.7
  67.7 0.5 collective-permute-start.6
  68.2 12.8 %front.7 = (f32[72,8,128]{2,1,0:T(8,128)}, f32[72,8,128]{2,1,0:T(8,128)}, f32[72,8,128]{2,1,0:T(8,128)}, f32[72,8,128]{2,1,0:T(8,128)}) custom-call(f32[36]{0:T(128)} %constant.21.clone.tab_ref, f32[2,36]{1,0:T(2,128)} %constant.24.clone.dir_ref, s32[1]{0:T(128)} %bitcast.2.pos_ref, s32[4,32,128]{2,1,0:T(8,128)} %bitcast.39, f32[32,128]{1,0:T(8,128)} %bitcast.45, ...), custom_call_target="tpu_custom_call" | custom-call | bytes 44000000 | tf_op jit(solution)/shard_map/front/pallas_call | solution.py:435
  81.0 0.0 collective-permute-done.8.refs_4_
  81.0 0.0 copy-start.6
  81.0 2.8 %collective-permute-start.11 = (f32[72,8,128]{2,1,0:T(8,128)}, f32[72,8,128]{2,1,0:T(8,128)S(1)}, u32[]{:S(2)}, u32[]{:S(2)}) collective-permute-start(f32[72,8,128]{2,1,0:T(8,128)} %get-tuple-element.74), channel_id=1, source_target_pairs={{0,3},{1,0},{2,1},{3,2},{4,7},{5,4},{6,5},{7,6},{8,11},{9,8},{10,9... | collective-permute-start | bytes 884744 | tf_op jit(solution)/shard_map/ppermute | solution.py:645
  83.8 19.2 %collective-permute-done.7.refs_3_ = f32[72,8,128]{2,1,0:T(8,128)S(1)} collective-permute-done((f32[72,8,128]{2,1,0:T(8,128)}, f32[72,8,128]{2,1,0:T(8,128)S(1)}, u32[]{:S(2)}, u32[]{:S(2)}) %collective-permute-start.7) | collective-permute-done | bytes 294944 | tf_op jit(solution)/shard_map/ppermute | solution.py:645
  103.0 0.0 collective-permute-start.10
  103.0 0.0 collective-permute-done.6.refs_2_
  103.0 0.0 copy-start.8
  103.0 0.1 collective-permute-start.9
  103.1 12.9 %front.8 = (f32[72,8,128]{2,1,0:T(8,128)}, f32[72,8,128]{2,1,0:T(8,128)}, f32[72,8,128]{2,1,0:T(8,128)}, f32[72,8,128]{2,1,0:T(8,128)}) custom-call(f32[36]{0:T(128)} %constant.21.clone.tab_ref, f32[2,36]{1,0:T(2,128)} %constant.24.clone.dir_ref, s32[1]{0:T(128)} %bitcast.2.pos_ref, s32[4,32,128]{2,1,0:T(8,128)} %bitcast.40, f32[32,128]{1,0:T(8,128)} %bitcast.46, ...), custom_call_target="tpu_custom_call" | custom-call | bytes 44000000 | tf_op jit(solution)/shard_map/front/pallas_call | solution.py:435
  116.0 0.0 copy-done.6
  116.0 0.0 copy-done.7
  116.0 0.0 copy-done.8
  116.0 0.0 collective-permute-done.11.refs_8_
  116.0 3.2 %collective-permute-start.14 = (f32[72,8,128]{2,1,0:T(8,128)}, f32[72,8,128]{2,1,0:T(8,128)S(1)}, u32[]{:S(2)}, u32[]{:S(2)}) collective-permute-start(f32[72,8,128]{2,1,0:T(8,128)} %get-tuple-element.82), channel_id=1, source_target_pairs={{0,3},{1,0},{2,1},{3,2},{4,7},{5,4},{6,5},{7,6},{8,11},{9,8},{10,9... | collective-permute-start | bytes 884744 | tf_op jit(solution)/shard_map/ppermute | solution.py:645
  119.2 0.0 collective-permute-done.10.refs_7_
  119.2 0.5 collective-permute-start.13
  119.7 0.0 collective-permute-done.9.refs_6_
  119.7 4.1 %collective-permute-start.12 = (f32[72,8,128]{2,1,0:T(8,128)}, f32[72,8,128]{2,1,0:T(8,128)S(1)}, u32[]{:S(2)}, u32[]{:S(2)}) collective-permute-start(f32[72,8,128]{2,1,0:T(8,128)} %get-tuple-element.78), channel_id=1, source_target_pairs={{0,1},{1,2},{2,3},{3,0},{4,5},{5,6},{6,7},{7,4},{8,9},{9,10},{10,1... | collective-permute-start | bytes 884744 | tf_op jit(solution)/shard_map/ppermute | solution.py:645
  123.8 12.9 %front.9 = (f32[72,8,128]{2,1,0:T(8,128)}, f32[72,8,128]{2,1,0:T(8,128)}, f32[72,8,128]{2,1,0:T(8,128)}, f32[72,8,128]{2,1,0:T(8,128)}) custom-call(f32[36]{0:T(128)} %constant.21.clone.tab_ref, f32[2,36]{1,0:T(2,128)} %constant.24.clone.dir_ref, s32[1]{0:T(128)} %bitcast.2.pos_ref, s32[4,32,128]{2,1,0:T(8,128)} %bitcast.41, f32[32,128]{1,0:T(8,128)} %bitcast.47, ...), custom_call_target="tpu_custom_call" | custom-call | bytes 44000000 | tf_op jit(solution)/shard_map/front/pallas_call | solution.py:435
  136.7 0.0 collective-permute-done.14.refs_12_
  136.7 0.1 collective-permute-start.17
  136.8 18.7 %collective-permute-done.13.refs_11_ = f32[72,8,128]{2,1,0:T(8,128)S(1)} collective-permute-done((f32[72,8,128]{2,1,0:T(8,128)}, f32[72,8,128]{2,1,0:T(8,128)S(1)}, u32[]{:S(2)}, u32[]{:S(2)}) %collective-permute-start.13) | collective-permute-done | bytes 294944 | tf_op jit(solution)/shard_map/ppermute | solution.py:645
  155.5 0.0 collective-permute-start.16
  155.5 0.0 collective-permute-done.12.refs_10_
  155.5 0.1 collective-permute-start.15
  155.6 0.7 copy.22
  156.4 0.3 copy.15
  156.6 0.9 reshape.42.spot_ref
  157.6 0.3 copy.16
  157.8 0.9 reshape.43.wts_ref
  158.8 1.3 dynamic-slice_bitcast_fusion.1.mask_ref
  160.1 0.0 collective-permute-done.17.refs_16_
  160.1 8.4 %collective-permute-done.16.refs_15_ = f32[72,8,128]{2,1,0:T(8,128)S(1)} collective-permute-done((f32[72,8,128]{2,1,0:T(8,128)}, f32[72,8,128]{2,1,0:T(8,128)S(1)}, u32[]{:S(2)}, u32[]{:S(2)}) %collective-permute-start.16) | collective-permute-done | bytes 294944 | tf_op jit(solution)/shard_map/ppermute | solution.py:645
  168.5 0.0 collective-permute-done.15.refs_14_
  168.5 0.7 copy-done.16
  169.2 0.1 copy-done.17
  169.3 23.2 %tail.1 = f32[1296,1024]{1,0:T(8,128)} custom-call(s32[5184]{0:T(1024)} %reshape.42.spot_ref, f32[2592]{0:T(1024)} %reshape.43.wts_ref, f32[3,36]{1,0:T(4,128)} %constant.22.clone.ftab_ref, f32[1296]{0:T(1024)} %constant.23.clone.frs_ref, f32[2,36]{1,0:T(2,128)} %constant.24.clone.dir_ref, s32[1]{0:T(128)} %bitcast.2.pos_ref, f32[2,8,128]{2,1,0:T(8,128)} %bitcast.65, ...), custom_call_target="tpu_custom_call" | custom-call | bytes 70000000 | tf_op jit(solution)/shard_map/tail/pallas_call | solution.py:550
  (33 shorter events, 0.1 us)
Async XLA Ops:
  0.0 155.6 %copy-start = (f32[2,4096]{1,0:T(2,128)S(1)}, f32[2,4096]{1,0:T(2,128)}, u32[]{:S(2)}) copy-start(f32[2,4096]{1,0:T(2,128)} %param.15) | copy-start | bytes 98308
  2.9 13.6 %collective-permute-start = (f32[1,592,128]{2,1,0:T(8,128)}, f32[1,592,128]{2,1,0:T(8,128)S(1)}, u32[]{:S(2)}, u32[]{:S(2)}) collective-permute-start(f32[1,592,128]{2,1,0:T(8,128)} %get-tuple-element.48), channel_id=1, source_target_pairs={{0,4},{4,8},{8,12},{1,5},{5,9},{9,13},{2,6},{6,10},{10,14},{3,7},{... | collective-permute-start | bytes 909320 | tf_op jit(solution)/shard_map/ppermute | solution.py:606
  7.4 19.2 %copy-start.18 = (s32[4,4096]{1,0:T(4,128)S(1)}, s32[4,4096]{1,0:T(4,128)}, u32[]{:S(2)}) copy-start(s32[4,4096]{1,0:T(4,128)} %param.17) | copy-start | bytes 196612
  7.5 9.1 %collective-permute-start.1 = (f32[1,592,128]{2,1,0:T(8,128)}, f32[1,592,128]{2,1,0:T(8,128)S(1)}, u32[]{:S(2)}, u32[]{:S(2)}) collective-permute-start(f32[1,592,128]{2,1,0:T(8,128)} %get-tuple-element.49), channel_id=1, source_target_pairs={{4,0},{8,4},{12,8},{5,1},{9,5},{13,9},{6,2},{10,6},{14,10},{7,3},{... | collective-permute-start | bytes 909320 | tf_op jit(solution)/shard_map/ppermute | solution.py:606
  16.5 10.8 %copy-start.4 = (f32[1,592,128]{2,1,0:T(8,128)}, f32[1,592,128]{2,1,0:T(8,128)S(1)}, u32[]{:S(2)}) copy-start(f32[1,592,128]{2,1,0:T(8,128)S(1)} %collective-permute-done.hs_ref) | copy-start | bytes 909316
  16.5 5.6 %copy-start.5 = (f32[1,592,128]{2,1,0:T(8,128)}, f32[1,592,128]{2,1,0:T(8,128)S(1)}, u32[]{:S(2)}) copy-start(f32[1,592,128]{2,1,0:T(8,128)S(1)} %collective-permute-done.1.hn_ref) | copy-start | bytes 909316
  16.5 30.4 %collective-permute-start.4 = (f32[8,592,128]{2,1,0:T(8,128)}, f32[8,592,128]{2,1,0:T(8,128)S(1)}, u32[]{:S(2)}, u32[]{:S(2)}) collective-permute-start(f32[8,592,128]{2,1,0:T(8,128)} %get-tuple-element.57), channel_id=1, source_target_pairs={{0,4},{4,8},{8,12},{1,5},{5,9},{9,13},{2,6},{6,10},{10,14},{3,7},{... | collective-permute-start | bytes 7274504 | tf_op jit(solution)/shard_map/ppermute | solution.py:606
  20.2 31.4 %collective-permute-start.5 = (f32[8,592,128]{2,1,0:T(8,128)}, f32[8,592,128]{2,1,0:T(8,128)}, u32[]{:S(2)}, u32[]{:S(2)}) collective-permute-start(f32[8,592,128]{2,1,0:T(8,128)} %get-tuple-element.58), channel_id=1, source_target_pairs={{4,0},{8,4},{12,8},{5,1},{9,5},{13,9},{6,2},{10,6},{14,10},{7,3},{... | collective-permute-start | bytes 7274504 | tf_op jit(solution)/shard_map/ppermute | solution.py:606
  22.1 15.4 %collective-permute-start.2 = (f32[1152,128]{1,0:T(8,128)}, f32[1152,128]{1,0:T(8,128)S(1)}, u32[]{:S(2)}, u32[]{:S(2)}) collective-permute-start(f32[1152,128]{1,0:T(8,128)} %get-tuple-element.52), channel_id=1, source_target_pairs={{0,1},{1,2},{2,3},{4,5},{5,6},{6,7},{8,9},{9,10},{10,11},{12,13},{... | collective-permute-start | bytes 1769480 | tf_op jit(solution)/shard_map/ppermute | solution.py:606
  25.4 16.3 %collective-permute-start.3 = (f32[1152,128]{1,0:T(8,128)}, f32[1152,128]{1,0:T(8,128)}, u32[]{:S(2)}, u32[]{:S(2)}) collective-permute-start(f32[1152,128]{1,0:T(8,128)} %get-tuple-element.53), channel_id=1, source_target_pairs={{1,0},{2,1},{3,2},{5,4},{6,5},{7,6},{9,8},{10,9},{11,10},{13,12},{... | collective-permute-start | bytes 1769480 | tf_op jit(solution)/shard_map/ppermute | solution.py:606
  37.5 4.1 %copy-start.3 = (f32[1152,128]{1,0:T(8,128)}, f32[1152,128]{1,0:T(8,128)S(1)}, u32[]{:S(2)}) copy-start(f32[1152,128]{1,0:T(8,128)S(1)} %collective-permute-done.2) | copy-start | bytes 1769476
  41.7 22.7 %all-to-all-start = ((f32[4,36,8,128]{3,2,1,0:T(8,128)}), f32[4,36,8,128]{3,2,1,0:T(8,128)S(1)}, u32[]{:S(2)}, u32[]{:S(2)}) async-start(f32[4,36,8,128]{3,2,1,0:T(8,128)} %front.5), calls=%async_computation | async-start | bytes 1179648 | tf_op jit(solution)/shard_map/all_to_all | solution.py:639
  47.0 4.6 %copy-start.1 = (f32[8,592,128]{2,1,0:T(8,128)}, f32[8,592,128]{2,1,0:T(8,128)S(1)}, u32[]{:S(2)}) copy-start(f32[8,592,128]{2,1,0:T(8,128)S(1)} %collective-permute-done.4.hs_ref) | copy-start | bytes 7274500
  64.4 16.6 %copy-start.2 = (f32[4,36,8,128]{3,2,1,0:T(8,128)}, f32[4,36,8,128]{3,2,1,0:T(8,128)S(1)}, u32[]{:S(2)}) copy-start(f32[4,36,8,128]{3,2,1,0:T(8,128)S(1)} %all-to-all-done.refs_0_) | copy-start | bytes 1769476
  64.4 16.6 %collective-permute-start.8 = (f32[72,8,128]{2,1,0:T(8,128)}, f32[72,8,128]{2,1,0:T(8,128)S(1)}, u32[]{:S(2)}, u32[]{:S(2)}) collective-permute-start(f32[72,8,128]{2,1,0:T(8,128)} %get-tuple-element.66), channel_id=1, source_target_pairs={{0,3},{1,0},{2,1},{3,2},{4,7},{5,4},{6,5},{7,6},{8,11},{9,8},{10,9... | collective-permute-start | bytes 884744 | tf_op jit(solution)/shard_map/ppermute | solution.py:645
  67.7 35.3 %collective-permute-start.7 = (f32[72,8,128]{2,1,0:T(8,128)}, f32[72,8,128]{2,1,0:T(8,128)S(1)}, u32[]{:S(2)}, u32[]{:S(2)}) collective-permute-start(f32[72,8,128]{2,1,0:T(8,128)} %get-tuple-element.64), channel_id=1, source_target_pairs={{0,2},{1,3},{2,0},{3,1},{4,6},{5,7},{6,4},{7,5},{8,10},{9,11},{10,... | collective-permute-start | bytes 884744 | tf_op jit(solution)/shard_map/ppermute | solution.py:645
  67.7 35.3 %collective-permute-start.6 = (f32[72,8,128]{2,1,0:T(8,128)}, f32[72,8,128]{2,1,0:T(8,128)S(1)}, u32[]{:S(2)}, u32[]{:S(2)}) collective-permute-start(f32[72,8,128]{2,1,0:T(8,128)} %get-tuple-element.62), channel_id=1, source_target_pairs={{0,1},{1,2},{2,3},{3,0},{4,5},{5,6},{6,7},{7,4},{8,9},{9,10},{10,1... | collective-permute-start | bytes 884744 | tf_op jit(solution)/shard_map/ppermute | solution.py:645
  81.0 35.0 %copy-start.6 = (f32[72,8,128]{2,1,0:T(8,128)}, f32[72,8,128]{2,1,0:T(8,128)S(1)}, u32[]{:S(2)}) copy-start(f32[72,8,128]{2,1,0:T(8,128)S(1)} %collective-permute-done.8.refs_4_) | copy-start | bytes 884740
  81.0 35.1 %collective-permute-start.11 = (f32[72,8,128]{2,1,0:T(8,128)}, f32[72,8,128]{2,1,0:T(8,128)S(1)}, u32[]{:S(2)}, u32[]{:S(2)}) collective-permute-start(f32[72,8,128]{2,1,0:T(8,128)} %get-tuple-element.74), channel_id=1, source_target_pairs={{0,3},{1,0},{2,1},{3,2},{4,7},{5,4},{6,5},{7,6},{8,11},{9,8},{10,9... | collective-permute-start | bytes 884744 | tf_op jit(solution)/shard_map/ppermute | solution.py:645
  103.0 13.0 %copy-start.7 = (f32[72,8,128]{2,1,0:T(8,128)}, f32[72,8,128]{2,1,0:T(8,128)S(1)}, u32[]{:S(2)}) copy-start(f32[72,8,128]{2,1,0:T(8,128)S(1)} %collective-permute-done.7.refs_3_) | copy-start | bytes 884740
  103.0 16.2 %collective-permute-start.10 = (f32[72,8,128]{2,1,0:T(8,128)}, f32[72,8,128]{2,1,0:T(8,128)S(1)}, u32[]{:S(2)}, u32[]{:S(2)}) collective-permute-start(f32[72,8,128]{2,1,0:T(8,128)} %get-tuple-element.72), channel_id=1, source_target_pairs={{0,2},{1,3},{2,0},{3,1},{4,6},{5,7},{6,4},{7,5},{8,10},{9,11},{10,... | collective-permute-start | bytes 884744 | tf_op jit(solution)/shard_map/ppermute | solution.py:645
  103.0 13.0 %copy-start.8 = (f32[72,8,128]{2,1,0:T(8,128)}, f32[72,8,128]{2,1,0:T(8,128)S(1)}, u32[]{:S(2)}) copy-start(f32[72,8,128]{2,1,0:T(8,128)S(1)} %collective-permute-done.6.refs_2_) | copy-start | bytes 884740
  103.0 16.7 %collective-permute-start.9 = (f32[72,8,128]{2,1,0:T(8,128)}, f32[72,8,128]{2,1,0:T(8,128)S(1)}, u32[]{:S(2)}, u32[]{:S(2)}) collective-permute-start(f32[72,8,128]{2,1,0:T(8,128)} %get-tuple-element.70), channel_id=1, source_target_pairs={{0,1},{1,2},{2,3},{3,0},{4,5},{5,6},{6,7},{7,4},{8,9},{9,10},{10,1... | collective-permute-start | bytes 884744 | tf_op jit(solution)/shard_map/ppermute | solution.py:645
  116.0 20.7 %copy-start.9 = (f32[72,8,128]{2,1,0:T(8,128)}, f32[72,8,128]{2,1,0:T(8,128)S(1)}, u32[]{:S(2)}) copy-start(f32[72,8,128]{2,1,0:T(8,128)S(1)} %collective-permute-done.11.refs_8_) | copy-start | bytes 884740
  116.0 20.7 %collective-permute-start.14 = (f32[72,8,128]{2,1,0:T(8,128)}, f32[72,8,128]{2,1,0:T(8,128)S(1)}, u32[]{:S(2)}, u32[]{:S(2)}) collective-permute-start(f32[72,8,128]{2,1,0:T(8,128)} %get-tuple-element.82), channel_id=1, source_target_pairs={{0,3},{1,0},{2,1},{3,2},{4,7},{5,4},{6,5},{7,6},{8,11},{9,8},{10,9... | collective-permute-start | bytes 884744 | tf_op jit(solution)/shard_map/ppermute | solution.py:645
  119.2 17.5 %copy-start.10 = (f32[72,8,128]{2,1,0:T(8,128)}, f32[72,8,128]{2,1,0:T(8,128)S(1)}, u32[]{:S(2)}) copy-start(f32[72,8,128]{2,1,0:T(8,128)S(1)} %collective-permute-done.10.refs_7_) | copy-start | bytes 884740
  119.2 36.3 %collective-permute-start.13 = (f32[72,8,128]{2,1,0:T(8,128)}, f32[72,8,128]{2,1,0:T(8,128)S(1)}, u32[]{:S(2)}, u32[]{:S(2)}) collective-permute-start(f32[72,8,128]{2,1,0:T(8,128)} %get-tuple-element.80), channel_id=1, source_target_pairs={{0,2},{1,3},{2,0},{3,1},{4,6},{5,7},{6,4},{7,5},{8,10},{9,11},{10,... | collective-permute-start | bytes 884744 | tf_op jit(solution)/shard_map/ppermute | solution.py:645
  119.7 17.0 %copy-start.11 = (f32[72,8,128]{2,1,0:T(8,128)}, f32[72,8,128]{2,1,0:T(8,128)S(1)}, u32[]{:S(2)}) copy-start(f32[72,8,128]{2,1,0:T(8,128)S(1)} %collective-permute-done.9.refs_6_) | copy-start | bytes 884740
  119.7 35.8 %collective-permute-start.12 = (f32[72,8,128]{2,1,0:T(8,128)}, f32[72,8,128]{2,1,0:T(8,128)S(1)}, u32[]{:S(2)}, u32[]{:S(2)}) collective-permute-start(f32[72,8,128]{2,1,0:T(8,128)} %get-tuple-element.78), channel_id=1, source_target_pairs={{0,1},{1,2},{2,3},{3,0},{4,5},{5,6},{6,7},{7,4},{8,9},{9,10},{10,1... | collective-permute-start | bytes 884744 | tf_op jit(solution)/shard_map/ppermute | solution.py:645
  123.8 32.5 %copy-start.19 = (s32[4,1296]{1,0:T(4,128)S(1)}, s32[4,1296]{1,0:T(4,128)}, u32[]{:S(2)}) copy-start(s32[4,1296]{1,0:T(4,128)} %param.22) | copy-start | bytes 62212
  123.8 33.8 %copy-start.20 = (f32[2,1296]{1,0:T(2,128)S(1)}, f32[2,1296]{1,0:T(2,128)}, u32[]{:S(2)}) copy-start(f32[2,1296]{1,0:T(2,128)} %param.23) | copy-start | bytes 31108
  136.7 31.7 %copy-start.12 = (f32[72,8,128]{2,1,0:T(8,128)}, f32[72,8,128]{2,1,0:T(8,128)S(1)}, u32[]{:S(2)}) copy-start(f32[72,8,128]{2,1,0:T(8,128)S(1)} %collective-permute-done.14.refs_12_) | copy-start | bytes 884740
  136.7 23.3 %collective-permute-start.17 = (f32[72,8,128]{2,1,0:T(8,128)}, f32[72,8,128]{2,1,0:T(8,128)S(1)}, u32[]{:S(2)}, u32[]{:S(2)}) collective-permute-start(f32[72,8,128]{2,1,0:T(8,128)} %get-tuple-element.90), channel_id=1, source_target_pairs={{0,3},{1,0},{2,1},{3,2},{4,7},{5,4},{6,5},{7,6},{8,11},{9,8},{10,9... | collective-permute-start | bytes 884744 | tf_op jit(solution)/shard_map/ppermute | solution.py:645
  155.5 13.0 %copy-start.13 = (f32[72,8,128]{2,1,0:T(8,128)}, f32[72,8,128]{2,1,0:T(8,128)S(1)}, u32[]{:S(2)}) copy-start(f32[72,8,128]{2,1,0:T(8,128)S(1)} %collective-permute-done.13.refs_11_) | copy-start | bytes 884740
  155.5 12.9 %collective-permute-start.16 = (f32[72,8,128]{2,1,0:T(8,128)}, f32[72,8,128]{2,1,0:T(8,128)S(1)}, u32[]{:S(2)}, u32[]{:S(2)}) collective-permute-start(f32[72,8,128]{2,1,0:T(8,128)} %get-tuple-element.88), channel_id=1, source_target_pairs={{0,2},{1,3},{2,0},{3,1},{4,6},{5,7},{6,4},{7,5},{8,10},{9,11},{10,... | collective-permute-start | bytes 884744 | tf_op jit(solution)/shard_map/ppermute | solution.py:645
  155.5 13.0 %copy-start.14 = (f32[72,8,128]{2,1,0:T(8,128)}, f32[72,8,128]{2,1,0:T(8,128)S(1)}, u32[]{:S(2)}) copy-start(f32[72,8,128]{2,1,0:T(8,128)S(1)} %collective-permute-done.12.refs_10_) | copy-start | bytes 884740
  155.5 12.9 %collective-permute-start.15 = (f32[72,8,128]{2,1,0:T(8,128)}, f32[72,8,128]{2,1,0:T(8,128)S(1)}, u32[]{:S(2)}, u32[]{:S(2)}) collective-permute-start(f32[72,8,128]{2,1,0:T(8,128)} %get-tuple-element.86), channel_id=1, source_target_pairs={{0,1},{1,2},{2,3},{3,0},{4,5},{5,6},{6,7},{7,4},{8,9},{9,10},{10,1... | collective-permute-start | bytes 884744 | tf_op jit(solution)/shard_map/ppermute | solution.py:645
  160.1 8.4 %copy-start.15 = (f32[72,8,128]{2,1,0:T(8,128)}, f32[72,8,128]{2,1,0:T(8,128)S(1)}, u32[]{:S(2)}) copy-start(f32[72,8,128]{2,1,0:T(8,128)S(1)} %collective-permute-done.17.refs_16_) | copy-start | bytes 884740
  168.5 0.7 copy-start.16
  168.5 0.8 copy-start.17

commit v4 on v2

--- a/solution.py
+++ b/solution.py
@@ -459,7 +459,7 @@
     nbins = nfreq * ND
     loads = []
     for c, chunk in enumerate(plan):
-        joined = c == 0
+        joined = False
         whole = next(parts) if joined else None
         for d in range(shares):
             part = whole.at[d] if joined else next(parts)
@@ -633,11 +633,11 @@
     order = pos
     for c, chunk in enumerate(plan):
         first, step, count = chunk
-        joined = c == 0
+        joined = False
         gi, slot = [(i, slots_of(g)[first]) for i, g in enumerate(groups) if chunk in g][0]
         ends = (low_in, high_in) if first == 0 else None
         blocks = front(speed, dirs, order, nbr, par, *halos[gi], slot, wet, ends, chunk, joined, shares, kmin, kmax)
-        earlier = sum(halos, ()) if c == 0 else arrived[0] if c == 1 else []
+        earlier = sum(halos, ()) if c == 0 else arrived[0][1:] if c == 1 else []
         order, *_ = lax.optimization_barrier((pos, blocks[0], *earlier))
         if joined:
             blocks, *_ = lax.optimization_barrier((blocks[0], low_in, high_in))
@@ -646,7 +646,8 @@
         here = [blocks[0]]
         for d in range(1, shares):
             rows = blocks[d]
-            rows, _ = lax.optimization_barrier((rows, arrived[-1][d if c > 1 else 0]))
+            before = [low_in, high_in] if c == 0 else arrived[0][1:] if c == 1 else [arrived[-1][d]]
+            rows, *_ = lax.optimization_barrier((rows, *before))
             here.append(lax.ppermute(rows, "bin", [(i, (i + d) % shares) for i in range(shares)]))
         arrived.append(here)
     parts = sum(arrived, [])

time: 189 us -> 191 us (1.011)
  waiting for transfers between devices: 28.5 us -> 39.8 us
  starting transfers between devices: 62.5 us -> 53.3 us
    ppermute x9 -> x12, waiting for transfers between devices: 13.9 us -> 33.1 us  [fast_on_device(): lax.ppermute(rows, 'bin', [(i, (i + d) % shares) for i in range(shares)])]
    all_to_all x1 -> x0, waiting for transfers between devices: 7.35 us -> none  [fast_on_device(): lax.all_to_all(blocks, 'bin', split_axis=0, concat_axis=0, tiled=True)]
    all_to_all x1 -> x0, starting transfers between devices: 5.65 us -> none  [fast_on_device(): lax.all_to_all(blocks, 'bin', split_axis=0, concat_axis=0, tiled=True)]
    ppermute x9 -> x12, starting transfers between devices: 39.1 us -> 36.9 us  [fast_on_device(): lax.ppermute(rows, 'bin', [(i, (i + d) % shares) for i in range(shares)])]
  transfers between devices with their start and end apart: 16 -> 18, of which waited for: 6 -> 7; matrix products, arithmetic and copies ran while one was open for 3% -> 3% of each run, Pallas kernels for 34% -> 33%
where the time goes in v4:
time: 191 us; the launch traced here: 189 us
  Pallas kernels  89.2 us (47%)
  starting transfers between devices  53.3 us (28%)
  waiting for transfers between devices  39.8 us (21%)
  local copies, waits for them, and re-layouts  6.72 us (4%)
    pallas_call x4, Pallas kernels, front(): pl.pallas_call(functools.partial(front_kernel, tiles, shares, nloc, kmin,...  56.1 us
    ppermute x12, starting transfers between devices, fast_on_device(): lax.ppermute(rows, 'bin', [(i, (i + d) % shares) for i in range(shares)])  36.9 us
    ppermute x12, waiting for transfers between devices, fast_on_device(): lax.ppermute(rows, 'bin', [(i, (i + d) % shares) for i in range(shares)])  33.1 us
    pallas_call x1, Pallas kernels, tail(): pl.pallas_call(functools.partial(tail_kernel, nfreq, bins_dev, plan), out...  23.2 us
    ppermute x6, starting transfers between devices, line(): return lax.ppermute(array, axis, pairs)  16.4 us
    pallas_call x2, Pallas kernels, prep(): pl.pallas_call(functools.partial(prep_kernel, points, bins, blocks, group...  9.91 us
    ppermute x6, waiting for transfers between devices, line(): return lax.ppermute(array, axis, pairs)  6.73 us
  transfers between devices with their start and end apart: 18, of which 7 were waited for; matrix products, arithmetic and copies ran while one was open for 3% of the time, Pallas kernels for 33%

profile of v4, /device:TPU:1, one launch (start us, length us, event | category | flops | bytes accessed | tf_op | source)
XLA Modules:
  0.0 189.4 jit_solution(4927149091604110048)
XLA Ops:
  0.0 0.0 copy-start
  0.0 3.2 %prep.2 = (f32[2,592,128]{2,1,0:T(8,128)}, f32[2,592,128]{2,1,0:T(8,128)}) custom-call(f32[324,4096]{1,0:T(8,128)} %spec_hbm.2, s32[1,4096]{1,0:T(1,128)} %bitcast.54), custom_call_target="tpu_custom_call" | custom-call | bytes 6000000 | tf_op jit(solution)/shard_map/prep/pallas_call | solution.py:300
  3.2 4.5 %collective-permute-start = (f32[2,592,128]{2,1,0:T(8,128)}, f32[2,592,128]{2,1,0:T(8,128)S(1)}, u32[]{:S(2)}, u32[]{:S(2)}) collective-permute-start(f32[2,592,128]{2,1,0:T(8,128)} %get-tuple-element.46), channel_id=1, source_target_pairs={{0,4},{4,8},{8,12},{1,5},{5,9},{9,13},{2,6},{6,10},{10,14},{3,7},{... | collective-permute-start | bytes 1818632 | tf_op jit(solution)/shard_map/ppermute | solution.py:611
  7.7 0.0 copy-start.16
  7.7 2.1 %collective-permute-start.1 = (f32[2,592,128]{2,1,0:T(8,128)}, f32[2,592,128]{2,1,0:T(8,128)S(1)}, u32[]{:S(2)}, u32[]{:S(2)}) collective-permute-start(f32[2,592,128]{2,1,0:T(8,128)} %get-tuple-element.47), channel_id=1, source_target_pairs={{4,0},{8,4},{12,8},{5,1},{9,5},{13,9},{6,2},{10,6},{14,10},{7,3},{... | collective-permute-start | bytes 1818632 | tf_op jit(solution)/shard_map/ppermute | solution.py:611
  9.8 6.8 %prep.3 = (f32[7,592,128]{2,1,0:T(8,128)}, f32[7,592,128]{2,1,0:T(8,128)}, f32[10368,128]{1,0:T(8,128)}, f32[1152,128]{1,0:T(8,128)}, f32[1152,128]{1,0:T(8,128)}) custom-call(f32[324,4096]{1,0:T(8,128)} %spec_hbm.2, s32[1,4096]{1,0:T(1,128)} %bitcast.55), custom_call_target="tpu_custom_call" | custom-call | bytes 27000000 | tf_op jit(solution)/shard_map/prep/pallas_call | solution.py:300
  16.5 0.0 collective-permute-done.hs_ref
  16.6 2.9 %collective-permute-done.1.hn_ref = f32[2,592,128]{2,1,0:T(8,128)S(1)} collective-permute-done((f32[2,592,128]{2,1,0:T(8,128)}, f32[2,592,128]{2,1,0:T(8,128)S(1)}, u32[]{:S(2)}, u32[]{:S(2)}) %collective-permute-start.1) | collective-permute-done | bytes 606240 | tf_op jit(solution)/shard_map/ppermute | solution.py:611
  19.4 1.9 %collective-permute-start.7 = (f32[7,592,128]{2,1,0:T(8,128)}, f32[7,592,128]{2,1,0:T(8,128)S(1)}, u32[]{:S(2)}, u32[]{:S(2)}) collective-permute-start(f32[7,592,128]{2,1,0:T(8,128)} %get-tuple-element.61), channel_id=1, source_target_pairs={{0,4},{4,8},{8,12},{1,5},{5,9},{9,13},{2,6},{6,10},{10,14},{3,7},{... | collective-permute-start | bytes 6365192 | tf_op jit(solution)/shard_map/ppermute | solution.py:611
  21.4 2.5 %collective-permute-start.8 = (f32[7,592,128]{2,1,0:T(8,128)}, f32[7,592,128]{2,1,0:T(8,128)}, u32[]{:S(2)}, u32[]{:S(2)}) collective-permute-start(f32[7,592,128]{2,1,0:T(8,128)} %get-tuple-element.62), channel_id=1, source_target_pairs={{4,0},{8,4},{12,8},{5,1},{9,5},{13,9},{6,2},{10,6},{14,10},{7,3},{... | collective-permute-start | bytes 6365192 | tf_op jit(solution)/shard_map/ppermute | solution.py:611
  23.9 4.1 %collective-permute-start.2 = (f32[1152,128]{1,0:T(8,128)}, f32[1152,128]{1,0:T(8,128)}, u32[]{:S(2)}, u32[]{:S(2)}) collective-permute-start(f32[1152,128]{1,0:T(8,128)} %get-tuple-element.52), channel_id=1, source_target_pairs={{0,1},{1,2},{2,3},{4,5},{5,6},{6,7},{8,9},{9,10},{10,11},{12,13},{... | collective-permute-start | bytes 1769480 | tf_op jit(solution)/shard_map/ppermute | solution.py:611
  28.0 1.3 collective-permute-start.3
  29.3 0.6 copy.21
  30.0 0.0 copy-done.3
  30.0 12.7 %front.4 = (f32[72,8,128]{2,1,0:T(8,128)}, f32[72,8,128]{2,1,0:T(8,128)}, f32[72,8,128]{2,1,0:T(8,128)}, f32[72,8,128]{2,1,0:T(8,128)}) custom-call(f32[36]{0:T(128)} %constant.21.clone.tab_ref, f32[2,36]{1,0:T(2,128)} %constant.24.clone.dir_ref, s32[1]{0:T(128)} %bitcast.2.pos_ref, s32[4,32,128]{2,1,0:T(8,128)} %bitcast.34, f32[32,128]{1,0:T(8,128)} %bitcast.38, ...), custom_call_target="tpu_custom_call" | custom-call | bytes 44000000 | tf_op jit(solution)/shard_map/front/pallas_call | solution.py:440
  42.7 0.0 collective-permute-done.2
  42.7 2.7 %collective-permute-done.3 = f32[1152,128]{1,0:T(8,128)} collective-permute-done((f32[1152,128]{1,0:T(8,128)}, f32[1152,128]{1,0:T(8,128)}, u32[]{:S(2)}, u32[]{:S(2)}) %collective-permute-start.3) | collective-permute-done | bytes 589856 | tf_op jit(solution)/shard_map/ppermute | solution.py:611
  45.4 1.5 collective-permute-start.6
  46.9 0.1 collective-permute-start.5
  47.0 1.3 collective-permute-start.4
  48.3 0.0 collective-permute-done.7.hs_ref
  48.3 1.1 collective-permute-done.8.hn_ref
  49.5 0.2 copy-done.1
  49.7 12.7 %front.5 = (f32[72,8,128]{2,1,0:T(8,128)}, f32[72,8,128]{2,1,0:T(8,128)}, f32[72,8,128]{2,1,0:T(8,128)}, f32[72,8,128]{2,1,0:T(8,128)}) custom-call(f32[36]{0:T(128)} %constant.21.clone.tab_ref, f32[2,36]{1,0:T(2,128)} %constant.24.clone.dir_ref, s32[1]{0:T(128)} %bitcast.2.pos_ref, s32[4,32,128]{2,1,0:T(8,128)} %bitcast.35, f32[32,128]{1,0:T(8,128)} %bitcast.39, ...), custom_call_target="tpu_custom_call" | custom-call | bytes 44000000 | tf_op jit(solution)/shard_map/front/pallas_call | solution.py:440
  62.4 0.0 collective-permute-done.6.refs_3_
  62.4 0.0 copy-start.7
  62.4 10.3 %collective-permute-done.5.refs_2_ = f32[72,8,128]{2,1,0:T(8,128)S(1)} collective-permute-done((f32[72,8,128]{2,1,0:T(8,128)}, f32[72,8,128]{2,1,0:T(8,128)S(1)}, u32[]{:S(2)}, u32[]{:S(2)}) %collective-permute-start.5) | collective-permute-done | bytes 294944 | tf_op jit(solution)/shard_map/ppermute | solution.py:651
  72.8 0.0 collective-permute-done.4.refs_1_
  72.8 0.1 collective-permute-start.11
  72.9 3.1 %collective-permute-start.10 = (f32[72,8,128]{2,1,0:T(8,128)}, f32[72,8,128]{2,1,0:T(8,128)S(1)}, u32[]{:S(2)}, u32[]{:S(2)}) collective-permute-start(f32[72,8,128]{2,1,0:T(8,128)} %get-tuple-element.68), channel_id=1, source_target_pairs={{0,2},{1,3},{2,0},{3,1},{4,6},{5,7},{6,4},{7,5},{8,10},{9,11},{10,... | collective-permute-start | bytes 884744 | tf_op jit(solution)/shard_map/ppermute | solution.py:651
  75.9 1.5 collective-permute-start.9
  77.4 17.8 %front.6 = (f32[108,8,128]{2,1,0:T(8,128)}, f32[108,8,128]{2,1,0:T(8,128)}, f32[108,8,128]{2,1,0:T(8,128)}, f32[108,8,128]{2,1,0:T(8,128)}) custom-call(f32[36]{0:T(128)} %constant.21.clone.tab_ref, f32[2,36]{1,0:T(2,128)} %constant.24.clone.dir_ref, s32[1]{0:T(128)} %bitcast.2.pos_ref, s32[4,32,128]{2,1,0:T(8,128)} %bitcast.36, f32[32,128]{1,0:T(8,128)} %bitcast.40, ...), custom_call_target="tpu_custom_call" | custom-call | bytes 66000000 | tf_op jit(solution)/shard_map/front/pallas_call | solution.py:440
  95.2 0.0 copy-done.7
  95.2 0.0 copy-done.8
  95.3 0.0 copy-done.9
  95.3 0.0 collective-permute-done.11.refs_7_
  95.3 1.8 collective-permute-start.14
  97.1 5.0 %collective-permute-done.10.refs_6_ = f32[72,8,128]{2,1,0:T(8,128)S(1)} collective-permute-done((f32[72,8,128]{2,1,0:T(8,128)}, f32[72,8,128]{2,1,0:T(8,128)S(1)}, u32[]{:S(2)}, u32[]{:S(2)}) %collective-permute-start.10) | collective-permute-done | bytes 294944 | tf_op jit(solution)/shard_map/ppermute | solution.py:651
  102.1 0.0 collective-permute-start.13
  102.1 0.0 collective-permute-done.9.refs_5_
  102.1 0.8 copy-done.12
  102.9 16.9 %collective-permute-start.12 = (f32[108,8,128]{2,1,0:T(8,128)}, f32[108,8,128]{2,1,0:T(8,128)S(1)}, u32[]{:S(2)}, u32[]{:S(2)}) collective-permute-start(f32[108,8,128]{2,1,0:T(8,128)} %get-tuple-element.74), channel_id=1, source_target_pairs={{0,1},{1,2},{2,3},{3,0},{4,5},{5,6},{6,7},{7,4},{8,9},{9,10},{10,1... | collective-permute-start | bytes 1327112 | tf_op jit(solution)/shard_map/ppermute | solution.py:651
  119.8 12.8 %front.7 = (f32[72,8,128]{2,1,0:T(8,128)}, f32[72,8,128]{2,1,0:T(8,128)}, f32[72,8,128]{2,1,0:T(8,128)}, f32[72,8,128]{2,1,0:T(8,128)}) custom-call(f32[36]{0:T(128)} %constant.21.clone.tab_ref, f32[2,36]{1,0:T(2,128)} %constant.24.clone.dir_ref, s32[1]{0:T(128)} %bitcast.2.pos_ref, s32[4,32,128]{2,1,0:T(8,128)} %bitcast.37, f32[32,128]{1,0:T(8,128)} %bitcast.41, ...), custom_call_target="tpu_custom_call" | custom-call | bytes 44000000 | tf_op jit(solution)/shard_map/front/pallas_call | solution.py:440
  132.6 0.0 copy-done.10
  132.6 0.0 copy-done.11
  132.6 0.0 collective-permute-done.14.refs_11_
  132.6 0.1 collective-permute-start.17
  132.7 7.4 %collective-permute-done.13.refs_10_ = f32[108,8,128]{2,1,0:T(8,128)S(1)} collective-permute-done((f32[108,8,128]{2,1,0:T(8,128)}, f32[108,8,128]{2,1,0:T(8,128)S(1)}, u32[]{:S(2)}, u32[]{:S(2)}) %collective-permute-start.13) | collective-permute-done | bytes 442400 | tf_op jit(solution)/shard_map/ppermute | solution.py:651
  140.1 0.0 collective-permute-start.16
  140.1 0.0 collective-permute-done.12.refs_9_
  140.1 10.6 %collective-permute-start.15 = (f32[72,8,128]{2,1,0:T(8,128)}, f32[72,8,128]{2,1,0:T(8,128)S(1)}, u32[]{:S(2)}, u32[]{:S(2)}) collective-permute-start(f32[72,8,128]{2,1,0:T(8,128)} %get-tuple-element.82), channel_id=1, source_target_pairs={{0,1},{1,2},{2,3},{3,0},{4,5},{5,6},{6,7},{7,4},{8,9},{9,10},{10,1... | collective-permute-start | bytes 884744 | tf_op jit(solution)/shard_map/ppermute | solution.py:651
  150.7 0.6 copy.22
  151.3 0.3 copy.15
  151.6 0.9 reshape.42.spot_ref
  152.5 0.3 copy.16
  152.8 0.9 reshape.43.wts_ref
  153.7 1.3 dynamic-slice_bitcast_fusion.1.mask_ref
  155.0 0.0 collective-permute-done.17.refs_15_
  155.0 10.3 %collective-permute-done.16.refs_14_ = f32[72,8,128]{2,1,0:T(8,128)S(1)} collective-permute-done((f32[72,8,128]{2,1,0:T(8,128)}, f32[72,8,128]{2,1,0:T(8,128)S(1)}, u32[]{:S(2)}, u32[]{:S(2)}) %collective-permute-start.16) | collective-permute-done | bytes 294944 | tf_op jit(solution)/shard_map/ppermute | solution.py:651
  165.3 0.0 collective-permute-done.15.refs_13_
  165.3 0.0 copy-done.5
  165.4 0.7 copy-done.14
  166.1 0.1 copy-done.15
  166.2 23.2 %tail.1 = f32[1296,1024]{1,0:T(8,128)} custom-call(s32[5184]{0:T(1024)} %reshape.42.spot_ref, f32[2592]{0:T(1024)} %reshape.43.wts_ref, f32[3,36]{1,0:T(4,128)} %constant.22.clone.ftab_ref, f32[1296]{0:T(1024)} %constant.23.clone.frs_ref, f32[2,36]{1,0:T(2,128)} %constant.24.clone.dir_ref, s32[1]{0:T(128)} %bitcast.2.pos_ref, f32[2,8,128]{2,1,0:T(8,128)} %bitcast.56, ...), custom_call_target="tpu_custom_call" | custom-call | bytes 70000000 | tf_op jit(solution)/shard_map/tail/pallas_call | solution.py:555
  (26 shorter events, 0.1 us)
Async XLA Ops:
  0.0 150.7 %copy-start = (f32[2,4096]{1,0:T(2,128)S(1)}, f32[2,4096]{1,0:T(2,128)}, u32[]{:S(2)}) copy-start(f32[2,4096]{1,0:T(2,128)} %param.15) | copy-start | bytes 98308
  3.2 13.4 %collective-permute-start = (f32[2,592,128]{2,1,0:T(8,128)}, f32[2,592,128]{2,1,0:T(8,128)S(1)}, u32[]{:S(2)}, u32[]{:S(2)}) collective-permute-start(f32[2,592,128]{2,1,0:T(8,128)} %get-tuple-element.46), channel_id=1, source_target_pairs={{0,4},{4,8},{8,12},{1,5},{5,9},{9,13},{2,6},{6,10},{10,14},{3,7},{... | collective-permute-start | bytes 1818632 | tf_op jit(solution)/shard_map/ppermute | solution.py:611
  7.7 21.6 %copy-start.16 = (s32[4,4096]{1,0:T(4,128)S(1)}, s32[4,4096]{1,0:T(4,128)}, u32[]{:S(2)}) copy-start(s32[4,4096]{1,0:T(4,128)} %param.17) | copy-start | bytes 196612
  7.7 11.7 %collective-permute-start.1 = (f32[2,592,128]{2,1,0:T(8,128)}, f32[2,592,128]{2,1,0:T(8,128)S(1)}, u32[]{:S(2)}, u32[]{:S(2)}) collective-permute-start(f32[2,592,128]{2,1,0:T(8,128)} %get-tuple-element.47), channel_id=1, source_target_pairs={{4,0},{8,4},{12,8},{5,1},{9,5},{13,9},{6,2},{10,6},{14,10},{7,3},{... | collective-permute-start | bytes 1818632 | tf_op jit(solution)/shard_map/ppermute | solution.py:611
  16.6 13.4 %copy-start.2 = (f32[2,592,128]{2,1,0:T(8,128)}, f32[2,592,128]{2,1,0:T(8,128)S(1)}, u32[]{:S(2)}) copy-start(f32[2,592,128]{2,1,0:T(8,128)S(1)} %collective-permute-done.hs_ref) | copy-start | bytes 1818628
  19.4 10.5 %copy-start.3 = (f32[2,592,128]{2,1,0:T(8,128)}, f32[2,592,128]{2,1,0:T(8,128)S(1)}, u32[]{:S(2)}) copy-start(f32[2,592,128]{2,1,0:T(8,128)S(1)} %collective-permute-done.1.hn_ref) | copy-start | bytes 1818628
  19.4 28.9 %collective-permute-start.7 = (f32[7,592,128]{2,1,0:T(8,128)}, f32[7,592,128]{2,1,0:T(8,128)S(1)}, u32[]{:S(2)}, u32[]{:S(2)}) collective-permute-start(f32[7,592,128]{2,1,0:T(8,128)} %get-tuple-element.61), channel_id=1, source_target_pairs={{0,4},{4,8},{8,12},{1,5},{5,9},{9,13},{2,6},{6,10},{10,14},{3,7},{... | collective-permute-start | bytes 6365192 | tf_op jit(solution)/shard_map/ppermute | solution.py:611
  21.4 28.1 %collective-permute-start.8 = (f32[7,592,128]{2,1,0:T(8,128)}, f32[7,592,128]{2,1,0:T(8,128)}, u32[]{:S(2)}, u32[]{:S(2)}) collective-permute-start(f32[7,592,128]{2,1,0:T(8,128)} %get-tuple-element.62), channel_id=1, source_target_pairs={{4,0},{8,4},{12,8},{5,1},{9,5},{13,9},{6,2},{10,6},{14,10},{7,3},{... | collective-permute-start | bytes 6365192 | tf_op jit(solution)/shard_map/ppermute | solution.py:611
  23.9 18.8 %collective-permute-start.2 = (f32[1152,128]{1,0:T(8,128)}, f32[1152,128]{1,0:T(8,128)}, u32[]{:S(2)}, u32[]{:S(2)}) collective-permute-start(f32[1152,128]{1,0:T(8,128)} %get-tuple-element.52), channel_id=1, source_target_pairs={{0,1},{1,2},{2,3},{4,5},{5,6},{6,7},{8,9},{9,10},{10,11},{12,13},{... | collective-permute-start | bytes 1769480 | tf_op jit(solution)/shard_map/ppermute | solution.py:611
  28.0 17.4 %collective-permute-start.3 = (f32[1152,128]{1,0:T(8,128)}, f32[1152,128]{1,0:T(8,128)}, u32[]{:S(2)}, u32[]{:S(2)}) collective-permute-start(f32[1152,128]{1,0:T(8,128)} %get-tuple-element.53), channel_id=1, source_target_pairs={{1,0},{2,1},{3,2},{5,4},{6,5},{7,6},{9,8},{10,9},{11,10},{13,12},{... | collective-permute-start | bytes 1769480 | tf_op jit(solution)/shard_map/ppermute | solution.py:611
  45.4 17.0 %collective-permute-start.6 = (f32[72,8,128]{2,1,0:T(8,128)}, f32[72,8,128]{2,1,0:T(8,128)S(1)}, u32[]{:S(2)}, u32[]{:S(2)}) collective-permute-start(f32[72,8,128]{2,1,0:T(8,128)} %get-tuple-element.58), channel_id=1, source_target_pairs={{0,3},{1,0},{2,1},{3,2},{4,7},{5,4},{6,5},{7,6},{8,11},{9,8},{10,9... | collective-permute-start | bytes 884744 | tf_op jit(solution)/shard_map/ppermute | solution.py:651
  46.9 25.9 %collective-permute-start.5 = (f32[72,8,128]{2,1,0:T(8,128)}, f32[72,8,128]{2,1,0:T(8,128)S(1)}, u32[]{:S(2)}, u32[]{:S(2)}) collective-permute-start(f32[72,8,128]{2,1,0:T(8,128)} %get-tuple-element.56), channel_id=1, source_target_pairs={{0,2},{1,3},{2,0},{3,1},{4,6},{5,7},{6,4},{7,5},{8,10},{9,11},{10,... | collective-permute-start | bytes 884744 | tf_op jit(solution)/shard_map/ppermute | solution.py:651
  47.0 25.8 %collective-permute-start.4 = (f32[72,8,128]{2,1,0:T(8,128)}, f32[72,8,128]{2,1,0:T(8,128)S(1)}, u32[]{:S(2)}, u32[]{:S(2)}) collective-permute-start(f32[72,8,128]{2,1,0:T(8,128)} %get-tuple-element.54), channel_id=1, source_target_pairs={{0,1},{1,2},{2,3},{3,0},{4,5},{5,6},{6,7},{7,4},{8,9},{9,10},{10,1... | collective-permute-start | bytes 884744 | tf_op jit(solution)/shard_map/ppermute | solution.py:651
  48.3 1.3 copy-start.1
  62.4 32.8 %copy-start.7 = (f32[72,8,128]{2,1,0:T(8,128)}, f32[72,8,128]{2,1,0:T(8,128)S(1)}, u32[]{:S(2)}) copy-start(f32[72,8,128]{2,1,0:T(8,128)S(1)} %collective-permute-done.6.refs_3_) | copy-start | bytes 884740
  72.8 22.5 %copy-start.8 = (f32[72,8,128]{2,1,0:T(8,128)}, f32[72,8,128]{2,1,0:T(8,128)S(1)}, u32[]{:S(2)}) copy-start(f32[72,8,128]{2,1,0:T(8,128)S(1)} %collective-permute-done.5.refs_2_) | copy-start | bytes 884740
  72.8 22.5 %copy-start.9 = (f32[72,8,128]{2,1,0:T(8,128)}, f32[72,8,128]{2,1,0:T(8,128)S(1)}, u32[]{:S(2)}) copy-start(f32[72,8,128]{2,1,0:T(8,128)S(1)} %collective-permute-done.4.refs_1_) | copy-start | bytes 884740
  72.8 22.5 %collective-permute-start.11 = (f32[72,8,128]{2,1,0:T(8,128)}, f32[72,8,128]{2,1,0:T(8,128)S(1)}, u32[]{:S(2)}, u32[]{:S(2)}) collective-permute-start(f32[72,8,128]{2,1,0:T(8,128)} %get-tuple-element.70), channel_id=1, source_target_pairs={{0,3},{1,0},{2,1},{3,2},{4,7},{5,4},{6,5},{7,6},{8,11},{9,8},{10,9... | collective-permute-start | bytes 884744 | tf_op jit(solution)/shard_map/ppermute | solution.py:651
  72.9 29.2 %collective-permute-start.10 = (f32[72,8,128]{2,1,0:T(8,128)}, f32[72,8,128]{2,1,0:T(8,128)S(1)}, u32[]{:S(2)}, u32[]{:S(2)}) collective-permute-start(f32[72,8,128]{2,1,0:T(8,128)} %get-tuple-element.68), channel_id=1, source_target_pairs={{0,2},{1,3},{2,0},{3,1},{4,6},{5,7},{6,4},{7,5},{8,10},{9,11},{10,... | collective-permute-start | bytes 884744 | tf_op jit(solution)/shard_map/ppermute | solution.py:651
  75.9 26.2 %collective-permute-start.9 = (f32[72,8,128]{2,1,0:T(8,128)}, f32[72,8,128]{2,1,0:T(8,128)S(1)}, u32[]{:S(2)}, u32[]{:S(2)}) collective-permute-start(f32[72,8,128]{2,1,0:T(8,128)} %get-tuple-element.66), channel_id=1, source_target_pairs={{0,1},{1,2},{2,3},{3,0},{4,5},{5,6},{6,7},{7,4},{8,9},{9,10},{10,1... | collective-permute-start | bytes 884744 | tf_op jit(solution)/shard_map/ppermute | solution.py:651
  95.3 37.3 %copy-start.10 = (f32[72,8,128]{2,1,0:T(8,128)}, f32[72,8,128]{2,1,0:T(8,128)S(1)}, u32[]{:S(2)}) copy-start(f32[72,8,128]{2,1,0:T(8,128)S(1)} %collective-permute-done.11.refs_7_) | copy-start | bytes 884740
  95.3 37.3 %collective-permute-start.14 = (f32[108,8,128]{2,1,0:T(8,128)}, f32[108,8,128]{2,1,0:T(8,128)S(1)}, u32[]{:S(2)}, u32[]{:S(2)}) collective-permute-start(f32[108,8,128]{2,1,0:T(8,128)} %get-tuple-element.78), channel_id=1, source_target_pairs={{0,3},{1,0},{2,1},{3,2},{4,7},{5,4},{6,5},{7,6},{8,11},{9,8},{10,9... | collective-permute-start | bytes 1327112 | tf_op jit(solution)/shard_map/ppermute | solution.py:651
  102.1 30.5 %copy-start.11 = (f32[72,8,128]{2,1,0:T(8,128)}, f32[72,8,128]{2,1,0:T(8,128)S(1)}, u32[]{:S(2)}) copy-start(f32[72,8,128]{2,1,0:T(8,128)S(1)} %collective-permute-done.10.refs_6_) | copy-start | bytes 884740
  102.1 38.0 %collective-permute-start.13 = (f32[108,8,128]{2,1,0:T(8,128)}, f32[108,8,128]{2,1,0:T(8,128)S(1)}, u32[]{:S(2)}, u32[]{:S(2)}) collective-permute-start(f32[108,8,128]{2,1,0:T(8,128)} %get-tuple-element.76), channel_id=1, source_target_pairs={{0,2},{1,3},{2,0},{3,1},{4,6},{5,7},{6,4},{7,5},{8,10},{9,11},{10,... | collective-permute-start | bytes 1327112 | tf_op jit(solution)/shard_map/ppermute | solution.py:651
  102.1 0.8 copy-start.12
  102.9 37.2 %collective-permute-start.12 = (f32[108,8,128]{2,1,0:T(8,128)}, f32[108,8,128]{2,1,0:T(8,128)S(1)}, u32[]{:S(2)}, u32[]{:S(2)}) collective-permute-start(f32[108,8,128]{2,1,0:T(8,128)} %get-tuple-element.74), channel_id=1, source_target_pairs={{0,1},{1,2},{2,3},{3,0},{4,5},{5,6},{6,7},{7,4},{8,9},{9,10},{10,1... | collective-permute-start | bytes 1327112 | tf_op jit(solution)/shard_map/ppermute | solution.py:651
  119.8 31.5 %copy-start.17 = (s32[4,1296]{1,0:T(4,128)S(1)}, s32[4,1296]{1,0:T(4,128)}, u32[]{:S(2)}) copy-start(s32[4,1296]{1,0:T(4,128)} %param.22) | copy-start | bytes 62212
  119.8 32.7 %copy-start.18 = (f32[2,1296]{1,0:T(2,128)S(1)}, f32[2,1296]{1,0:T(2,128)}, u32[]{:S(2)}) copy-start(f32[2,1296]{1,0:T(2,128)} %param.23) | copy-start | bytes 31108
  132.6 32.7 %copy-start.4 = (f32[108,8,128]{2,1,0:T(8,128)}, f32[108,8,128]{2,1,0:T(8,128)S(1)}, u32[]{:S(2)}) copy-start(f32[108,8,128]{2,1,0:T(8,128)S(1)} %collective-permute-done.14.refs_11_) | copy-start | bytes 1327108
  132.6 22.4 %collective-permute-start.17 = (f32[72,8,128]{2,1,0:T(8,128)}, f32[72,8,128]{2,1,0:T(8,128)S(1)}, u32[]{:S(2)}, u32[]{:S(2)}) collective-permute-start(f32[72,8,128]{2,1,0:T(8,128)} %get-tuple-element.86), channel_id=1, source_target_pairs={{0,3},{1,0},{2,1},{3,2},{4,7},{5,4},{6,5},{7,6},{8,11},{9,8},{10,9... | collective-permute-start | bytes 884744 | tf_op jit(solution)/shard_map/ppermute | solution.py:651
  140.1 25.3 %copy-start.5 = (f32[108,8,128]{2,1,0:T(8,128)}, f32[108,8,128]{2,1,0:T(8,128)S(1)}, u32[]{:S(2)}) copy-start(f32[108,8,128]{2,1,0:T(8,128)S(1)} %collective-permute-done.13.refs_10_) | copy-start | bytes 1327108
  140.1 25.3 %collective-permute-start.16 = (f32[72,8,128]{2,1,0:T(8,128)}, f32[72,8,128]{2,1,0:T(8,128)S(1)}, u32[]{:S(2)}, u32[]{:S(2)}) collective-permute-start(f32[72,8,128]{2,1,0:T(8,128)} %get-tuple-element.84), channel_id=1, source_target_pairs={{0,2},{1,3},{2,0},{3,1},{4,6},{5,7},{6,4},{7,5},{8,10},{9,11},{10,... | collective-permute-start | bytes 884744 | tf_op jit(solution)/shard_map/ppermute | solution.py:651
  140.1 25.3 %copy-start.6 = (f32[108,8,128]{2,1,0:T(8,128)}, f32[108,8,128]{2,1,0:T(8,128)S(1)}, u32[]{:S(2)}) copy-start(f32[108,8,128]{2,1,0:T(8,128)S(1)} %collective-permute-done.12.refs_9_) | copy-start | bytes 1327108
  140.1 25.3 %collective-permute-start.15 = (f32[72,8,128]{2,1,0:T(8,128)}, f32[72,8,128]{2,1,0:T(8,128)S(1)}, u32[]{:S(2)}, u32[]{:S(2)}) collective-permute-start(f32[72,8,128]{2,1,0:T(8,128)} %get-tuple-element.82), channel_id=1, source_target_pairs={{0,1},{1,2},{2,3},{3,0},{4,5},{5,6},{6,7},{7,4},{8,9},{9,10},{10,1... | collective-permute-start | bytes 884744 | tf_op jit(solution)/shard_map/ppermute | solution.py:651
  155.0 10.4 %copy-start.13 = (f32[72,8,128]{2,1,0:T(8,128)}, f32[72,8,128]{2,1,0:T(8,128)S(1)}, u32[]{:S(2)}) copy-start(f32[72,8,128]{2,1,0:T(8,128)S(1)} %collective-permute-done.17.refs_15_) | copy-start | bytes 884740
  165.3 0.7 copy-start.14
  165.3 0.8 copy-start.15
